TPU v7x, 32 devices: a whole 2x2x4 slice. The times are simulated.
32 devices in a mesh: pipe: 2 (over core), expert: 16 (over z, y, x).
Axes of the slice: x: 2, y: 2, z: 4, core: 2. Of those that a mesh axis runs over, the one named last changes fastest.
Arguments:
- section_inputs: bfloat16 [2, 2048, 7168], P('pipe', 'expert'), may hold values from -6 to 6
- output_grads: bfloat16 [2, 2048, 7168], P('pipe', 'expert'), may hold values from -6 to 6
- w_gate: bfloat16 [2, 7168, 2048], P('pipe', None, 'expert'), may hold values from -0.0625 to 0.0625
- w_up: bfloat16 [2, 7168, 2048], P('pipe', None, 'expert'), may hold values from -0.0625 to 0.0625
- w_down: bfloat16 [2, 2048, 7168], P('pipe', 'expert'), may hold values from -0.125 to 0.125
- route_ids: int32 [2, 2048, 8], P('pipe', 'expert'), may hold values from 0 to 255, all different within a row; in each aligned block of 128 rows (0 to 127, 128 to 255, ..., all dimensions but the last counted through in order) at most 5 rows name the same one
- route_gates: float32 [2, 2048, 8], P('pipe', 'expert'), may hold values from 0.25 to 1
Outputs:
- handed_grads: bfloat16 [2, 2048, 7168], P('pipe', 'expert')
- down_grads: bfloat16 [2, 2048, 7168], P('pipe', 'expert')
Inputs may be any that keep to these rules, and one draw needn't show every extreme that they name: `route_ids`: each row names 8 different experts. Within the 128 rows of one device of one section, no expert is named by more than 5 rows.
All inputs are finite; a program needn't handle non-finite values.
Results may differ from a plain program's by a relative error of at most 0.0057.
Values may be sent and summed in bfloat16 or wider, within the bound.
A program may use at most 192 MiB of HBM per device.

v0:
```python
import jax
import jax.numpy as jnp
from jax import lax
from jax.sharding import PartitionSpec as P

SHARDS = 16
CAP = 5


def from_behind(value, axis, steps):
    count = lax.axis_size(axis)
    pairs = [(source, (source + steps) % count) for source in range(count)]
    return lax.ppermute(value, axis, pairs)


def expert_work(rows_in, rows_grad, gate_cols, up_cols, down_rows):
    count, slots, model_width = rows_in.shape
    flat_in = rows_in.reshape(count * slots, model_width)
    flat_grad = rows_grad.reshape(count * slots, model_width)
    gate_pre = jnp.dot(flat_in, gate_cols, preferred_element_type=jnp.float32)
    up_pre = jnp.dot(flat_in, up_cols, preferred_element_type=jnp.float32)
    sigma = jax.nn.sigmoid(gate_pre)
    silu_gate = gate_pre * sigma
    hidden = (silu_gate * up_pre).astype(jnp.bfloat16)
    contract = (((1,), (1,)), ((), ()))
    back_hidden = lax.dot_general(
        flat_grad, down_rows, contract, preferred_element_type=jnp.float32
    )
    grad_gate = (back_hidden * up_pre * sigma * (1.0 + gate_pre * (1.0 - sigma))).astype(
        jnp.bfloat16
    )
    grad_up = (back_hidden * silu_gate).astype(jnp.bfloat16)
    partial_value = lax.dot_general(
        grad_gate, gate_cols, contract, preferred_element_type=jnp.float32
    )
    partial_value = partial_value + lax.dot_general(
        grad_up, up_cols, contract, preferred_element_type=jnp.float32
    )
    return (
        partial_value.astype(jnp.bfloat16).reshape(count, slots, model_width),
        hidden.reshape(count, slots, -1),
    )


def body(section_inputs, output_grads, w_gate, w_up, w_down, route_ids, route_gates):
    inputs = section_inputs[0]
    grads = output_grads[0]
    route = route_ids[0]
    gate = route_gates[0]
    gate_cols = w_gate[0]
    up_cols = w_up[0]
    down_rows = w_down[0]
    tok_rows, model_width = inputs.shape
    block_width = gate_cols.shape[1]
    width = lax.axis_size("expert")
    live_count = width // SHARDS
    slot_count = CAP
    expert_ids = jnp.arange(live_count, dtype=jnp.int32)
    hit = route[:, :, None] == expert_ids
    member = jnp.sum(hit.astype(jnp.int32), axis=1)
    weight = jnp.sum(jnp.where(hit, gate[:, :, None], 0.0), axis=1)
    position = jnp.cumsum(member, axis=0) - member
    slot_ids = jnp.arange(slot_count, dtype=jnp.int32)
    pick = (member[:, :, None] == 1) & (position[:, :, None] == slot_ids)
    pick_mat = pick.astype(jnp.bfloat16).reshape(tok_rows, live_count * slot_count)
    rows_first = (((0,), (0,)), ((), ()))
    rows_in = lax.dot_general(
        pick_mat, inputs, rows_first, preferred_element_type=jnp.float32
    ).astype(jnp.bfloat16)
    chosen_grads = lax.dot_general(pick_mat, grads, rows_first, preferred_element_type=jnp.float32)
    slot_gate = jnp.sum(pick.astype(jnp.float32) * weight[:, :, None], axis=0).reshape(
        live_count * slot_count, 1
    )
    rows_grad = (chosen_grads * slot_gate).astype(jnp.bfloat16)
    send_in = jnp.broadcast_to(
        rows_in.reshape(live_count, 1, slot_count, model_width),
        (live_count, SHARDS, slot_count, model_width),
    ).reshape(width, slot_count, model_width)
    send_grad = jnp.broadcast_to(
        rows_grad.reshape(live_count, 1, slot_count, model_width),
        (live_count, SHARDS, slot_count, model_width),
    ).reshape(width, slot_count, model_width)
    got_in, got_grad = (
        lax.all_to_all(send_in, "expert", split_axis=0, concat_axis=0, tiled=True),
        lax.all_to_all(send_grad, "expert", split_axis=0, concat_axis=0, tiled=True),
    )
    partial_value, hidden = expert_work(got_in, got_grad, gate_cols, up_cols, down_rows)
    returned = lax.all_to_all(partial_value, "expert", split_axis=0, concat_axis=0, tiled=True)
    down_part = lax.dot_general(
        hidden.reshape(-1, block_width),
        got_grad.reshape(-1, model_width),
        rows_first,
        preferred_element_type=jnp.float32,
    ).astype(jnp.bfloat16)
    full_pick = jnp.broadcast_to(pick[:, :, None, :], (tok_rows, live_count, SHARDS, slot_count))
    full_pick = full_pick.astype(jnp.bfloat16).reshape(tok_rows, width * slot_count)
    branch = jnp.dot(
        full_pick,
        returned.reshape(width * slot_count, model_width),
        preferred_element_type=jnp.float32,
    )
    input_grad = (grads.astype(jnp.float32) + branch).astype(jnp.bfloat16)
    handed = from_behind(input_grad, "pipe", -1)
    return (handed[None], down_part[None])


def solution(mesh):
    return jax.shard_map(
        body,
        mesh=mesh,
        in_specs=(
            P("pipe", "expert", None),
            P("pipe", "expert", None),
            P("pipe", None, "expert"),
            P("pipe", None, "expert"),
            P("pipe", "expert", None),
            P("pipe", "expert", None),
            P("pipe", "expert", None),
        ),
        out_specs=(P("pipe", "expert", None), P("pipe", "expert", None)),
        check_vma=False,
    )
```

profile of v0, /device:TPU:13, one launch (start us, length us, event | category | flops | bytes accessed | tf_op | source)
XLA Modules:
  0.0 168.7 jit_solution(606558764149105898)
XLA Ops:
  0.6 0.0 copy-start
  0.6 0.9 select_reduce_fusion
  1.5 0.1 copy.15
  1.6 0.2 reduce-window.7
  1.8 0.1 reduce.5
  1.9 1.8 %convolution_convert_fusion.1 = bf16[5,7168]{1,0:T(8,128)(2,1)S(1)} fusion(bf16[1,128,7168]{2,1,0:T(8,128)(2,1)} %param.7, s32[128]{0:T(128)S(1)} %sub.12, pred[128]{0:T(512)(128)(4,1)S(1)} %broadcast_compare_fusion.1), kind=kOutput, calls=%fused_computation.9 | convolution fusion | flops 9212160 | bytes 1907328 | tf_op jit(solution)/shard_map/dot_general | solution.py:67
  3.8 1.4 reshape.268
  5.2 6.6 %all-to-all-start.1 = ((bf16[16,5,7168]{2,1,0:T(8,128)(2,1)}), bf16[16,5,7168]{2,1,0:T(8,128)(2,1)}, u32[]{:S(2)}, u32[]{:S(2)}) async-start(bf16[16,5,7168]{2,1,0:T(8,128)(2,1)} %reshape.268), calls=%async_computation.1 | async-start | bytes 3670016 | tf_op jit(solution)/shard_map/all_to_all | solution.py:84
  11.8 0.1 fusion.27
  11.9 1.8 %fusion.4 = bf16[5,7168]{1,0:T(8,128)(2,1)S(1)} fusion(bf16[1,128,7168]{2,1,0:T(8,128)(2,1)} %param.8, f32[5]{0:T(128)S(1)} %fusion.27, s32[128]{0:T(128)S(1)} %sub.12, pred[128]{0:T(512)(128)(4,1)S(1)} %broadcast_compare_fusion.1), kind=kOutput, calls=%fused_computation.8 | convolution fusion | flops 9248000 | bytes 1907348 | tf_op jit(solution)/shard_map/dot_general | solution.py:70
  13.8 40.5 %all-to-all-done.1 = bf16[16,5,7168]{2,1,0:T(8,128)(2,1)} async-done(((bf16[16,5,7168]{2,1,0:T(8,128)(2,1)}), bf16[16,5,7168]{2,1,0:T(8,128)(2,1)}, u32[]{:S(2)}, u32[]{:S(2)}) %all-to-all-start.1) | async-done | bytes 1146912 | tf_op jit(solution)/shard_map/all_to_all | solution.py:84
  54.3 1.4 reshape.266
  55.7 4.3 %all-to-all-start = ((bf16[16,5,7168]{2,1,0:T(8,128)(2,1)}), bf16[16,5,7168]{2,1,0:T(8,128)(2,1)}, u32[]{:S(2)}, u32[]{:S(2)}) async-start(bf16[16,5,7168]{2,1,0:T(8,128)(2,1)} %reshape.266), calls=%async_computation | async-start | bytes 3670016 | tf_op jit(solution)/shard_map/all_to_all | solution.py:85
  60.0 1.7 %reshape.269 = bf16[80,7168]{1,0:T(8,128)(2,1)S(1)} reshape(bf16[16,5,7168]{2,1,0:T(8,128)(2,1)} %all-to-all-done.1) | data formatting | bytes 2293760 | tf_op jit(solution)/shard_map/reshape | solution.py:18
  61.8 0.0 copy-start.1
  61.8 0.5 fusion.7
  62.3 1.0 copy-done.1
  63.3 0.5 fusion.10
  63.8 38.9 %all-to-all-done = bf16[16,5,7168]{2,1,0:T(8,128)(2,1)} async-done(((bf16[16,5,7168]{2,1,0:T(8,128)(2,1)}), bf16[16,5,7168]{2,1,0:T(8,128)(2,1)}, u32[]{:S(2)}, u32[]{:S(2)}) %all-to-all-start) | async-done | bytes 1146912 | tf_op jit(solution)/shard_map/all_to_all | solution.py:85
  102.7 1.7 %reshape.267 = bf16[80,7168]{1,0:T(8,128)(2,1)S(1)} reshape(bf16[16,5,7168]{2,1,0:T(8,128)(2,1)} %all-to-all-done) | data formatting | bytes 2293760 | tf_op jit(solution)/shard_map/reshape | solution.py:19
  104.4 2.2 %fusion.13 = f32[80,128]{1,0:T(8,128)S(1)} fusion(bf16[80,7168]{1,0:T(8,128)(2,1)S(1)} %reshape.267, bf16[1,128,7168]{2,1,0:T(8,128)(2,1)} %param.11), kind=kOutput, calls=%fused_computation.18 | convolution fusion | flops 146800640 | bytes 3022848 | tf_op jit(solution)/shard_map/dot_general | solution.py:26
  106.7 0.8 fusion.5
  107.5 0.7 copy-done.2
  108.2 1.8 %fusion.3 = bf16[80,7168]{1,0:T(8,128)(2,1)} fusion(f32[80,7168]{1,0:T(8,128)S(1)} %fusion.5, bf16[1,7168,128]{2,1,0:T(8,128)(2,1)S(1)} %copy-done.2, f32[80,128]{1,0:T(8,128)S(1)} %fusion.13, f32[80,128]{1,0:T(8,128)S(1)} %fusion.7), kind=kOutput, calls=%fused_computation.6 | convolution fusion | flops 148008960 | bytes 5357568 | tf_op jit(solution)/shard_map/dot_general | solution.py:36
  110.0 2.5 %reshape.270 = bf16[16,5,7168]{2,1,0:T(8,128)(2,1)} reshape(bf16[80,7168]{1,0:T(8,128)(2,1)} %fusion.3) | data formatting | bytes 2293760 | tf_op jit(solution)/shard_map/reshape | solution.py:40
  112.5 4.3 %all-to-all-start.2 = ((bf16[16,5,7168]{2,1,0:T(8,128)(2,1)}), bf16[16,5,7168]{2,1,0:T(8,128)(2,1)}, u32[]{:S(2)}, u32[]{:S(2)}) async-start(bf16[16,5,7168]{2,1,0:T(8,128)(2,1)} %reshape.270), calls=%async_computation.2 | async-start | bytes 3670016 | tf_op jit(solution)/shard_map/all_to_all | solution.py:88
  116.8 42.3 %all-to-all-done.2 = bf16[16,5,7168]{2,1,0:T(8,128)(2,1)} async-done(((bf16[16,5,7168]{2,1,0:T(8,128)(2,1)}), bf16[16,5,7168]{2,1,0:T(8,128)(2,1)}, u32[]{:S(2)}, u32[]{:S(2)}) %all-to-all-start.2) | async-done | bytes 1146912 | tf_op jit(solution)/shard_map/all_to_all | solution.py:88
  159.2 3.3 %fusion.1 = bf16[128,7168]{1,0:T(8,128)(2,1)S(1)} fusion(bf16[1,128,7168]{2,1,0:T(8,128)(2,1)} %param.8, bf16[16,5,7168]{2,1,0:T(8,128)(2,1)} %all-to-all-done.2, pred[128,5]{0,1:T(8,128)(4,1)S(1)} %fusion.22), kind=kOutput, calls=%fused_computation.2 | convolution fusion | flops 149553152 | bytes 4817536 | tf_op jit(solution)/shard_map/dot_general | solution.py:97
  162.5 1.5 collective-permute-start
  164.1 1.9 %fusion.2 = bf16[1,128,7168]{2,1,0:T(8,128)(2,1)} fusion(bf16[80,7168]{1,0:T(8,128)(2,1)S(1)} %reshape.267, f32[80,128]{1,0:T(8,128)S(1)} %fusion.10, f32[80,128]{1,0:T(8,128)S(1)} %fusion.7), kind=kOutput, calls=%fused_computation.5 | convolution fusion | flops 147779584 | bytes 3063808 | tf_op jit(solution)/shard_map/dot_general | solution.py:89
  166.0 1.5 collective-permute-done
  167.5 1.2 copy.20
  (6 shorter events, 0.0 us)
Async XLA Ops:
  0.6 61.2 %copy-start = (bf16[1,7168,128]{2,1,0:T(8,128)(2,1)S(1)}, bf16[1,7168,128]{2,1,0:T(8,128)(2,1)}, u32[]{:S(2)}) copy-start(bf16[1,7168,128]{2,1,0:T(8,128)(2,1)} %param.9) | copy-start | bytes 5505028
  5.2 49.1 %all-to-all-start.1 = ((bf16[16,5,7168]{2,1,0:T(8,128)(2,1)}), bf16[16,5,7168]{2,1,0:T(8,128)(2,1)}, u32[]{:S(2)}, u32[]{:S(2)}) async-start(bf16[16,5,7168]{2,1,0:T(8,128)(2,1)} %reshape.268), calls=%async_computation.1 | async-start | bytes 3670016 | tf_op jit(solution)/shard_map/all_to_all | solution.py:84
  55.7 47.0 %all-to-all-start = ((bf16[16,5,7168]{2,1,0:T(8,128)(2,1)}), bf16[16,5,7168]{2,1,0:T(8,128)(2,1)}, u32[]{:S(2)}, u32[]{:S(2)}) async-start(bf16[16,5,7168]{2,1,0:T(8,128)(2,1)} %reshape.266), calls=%async_computation | async-start | bytes 3670016 | tf_op jit(solution)/shard_map/all_to_all | solution.py:85
  61.8 1.5 copy-start.1
  106.7 1.5 copy-start.2
  112.5 46.7 %all-to-all-start.2 = ((bf16[16,5,7168]{2,1,0:T(8,128)(2,1)}), bf16[16,5,7168]{2,1,0:T(8,128)(2,1)}, u32[]{:S(2)}, u32[]{:S(2)}) async-start(bf16[16,5,7168]{2,1,0:T(8,128)(2,1)} %reshape.270), calls=%async_computation.2 | async-start | bytes 3670016 | tf_op jit(solution)/shard_map/all_to_all | solution.py:88
  162.5 5.0 %collective-permute-start = (bf16[128,7168]{1,0:T(8,128)(2,1)S(1)}, bf16[128,7168]{1,0:T(8,128)(2,1)S(1)}, u32[]{:S(2)}, u32[]{:S(2)}) collective-permute-start(bf16[128,7168]{1,0:T(8,128)(2,1)S(1)} %fusion.1), channel_id=1, source_target_pairs={{0,16},{16,0},{1,17},{17,1},{2,18},{18,2},{3,19},{19,3},{4,20},{20... | collective-permute-start | bytes 5505032 | tf_op jit(solution)/shard_map/ppermute | solution.py:13
where the time goes:
time: 169 us
  waiting for transfers between devices  123 us (73%)
  starting transfers between devices  16.8 us (10%)
  matrix products  14.6 us (9%)
  local copies, waits for them, and re-layouts  12 us (7%)
    all_to_all x1, waiting for transfers between devices, body(): lax.all_to_all(partial_value, 'expert', split_axis=0, concat_axis=0, tile...  42.3 us
    all_to_all x1, waiting for transfers between devices, body(): lax.all_to_all(send_in, 'expert', split_axis=0, concat_axis=0, tiled=True)  40.5 us
    all_to_all x1, waiting for transfers between devices, body(): lax.all_to_all(send_grad, 'expert', split_axis=0, concat_axis=0, tiled=True)  38.9 us
    all_to_all x1, starting transfers between devices, body(): lax.all_to_all(send_in, 'expert', split_axis=0, concat_axis=0, tiled=True)  6.61 us
    all_to_all x1, starting transfers between devices, body(): lax.all_to_all(send_grad, 'expert', split_axis=0, concat_axis=0, tiled=True)  4.32 us
    all_to_all x1, starting transfers between devices, body(): lax.all_to_all(partial_value, 'expert', split_axis=0, concat_axis=0, tile...  4.32 us
  transfers between devices with their start and end apart: 4, of which 4 were waited for; matrix products, arithmetic and copies ran while one was open for 4% of the time, Pallas kernels for 0%

commit v1 on v0

v1 whole, which is shorter than its diff:
```python
import jax
import jax.numpy as jnp
from jax import lax
from jax.experimental import pallas as pl
from jax.experimental.pallas import tpu as pltpu
from jax.sharding import PartitionSpec as P

SHARDS = 16
CAP = 5
PIECES = 8
MESH = pl.DeviceIdType.MESH
CONTRACT_LAST = (((1,), (1,)), ((), ()))
ROWS_FIRST = (((0,), (0,)), ((), ()))


def hidden_grads(gate_pre, up_pre, back_hidden):
    sigma = jax.nn.sigmoid(gate_pre)
    silu_gate = gate_pre * sigma
    hidden = silu_gate * up_pre
    grad_gate = back_hidden * up_pre * sigma * (1.0 + gate_pre * (1.0 - sigma))
    grad_up = back_hidden * silu_gate
    return hidden, grad_gate, grad_up


def flip(z, k):
    if k == 0:
        return z
    if k == 1:
        return z + 1 - 2 * lax.rem(z, 2)
    if k == 2:
        return lax.rem(z + 2, 4)
    return 3 - z


def group_kernel(
    x_hbm, g_hbm, wg_hbm, wu_hbm, wd_hbm, route_ref, gate_ref, perm_ref, unperm_ref,
    rows_out, down_out,
    x_v, g_v, wgu, wd_v, staged, plain, plain_in, gath, xf, gf, pfull, part, diag_in,
    fwd_x, fwd_y, in_x, in_y, zsum, in_z, down_v, rows_v,
    load_sem, out_sem, z_send, z_recv, xy_send, xy_recv, d_send, d_recv, p_send, p_recv,
    s1_send, s1_recv, s2_send, s2_recv, s3_send, s3_recv,
):
    slots, piece = staged.shape[0], staged.shape[2]
    block = wd_v.shape[0]
    pipe = lax.axis_index("pipe")
    me = lax.axis_index("expert")
    base = (me // SHARDS) * SHARDS
    local = lax.rem(me, SHARDS)
    z = local // 4
    xy = lax.rem(local, 4)
    y, x = xy // 2, lax.rem(xy, 2)
    at_x, at_y, at_d = y * 2 + 1 - x, (1 - y) * 2 + x, 3 - xy

    def device(p, zz, spot):
        return {"pipe": p, "expert": base + zz * 4 + spot}

    x_dev, y_dev = device(pipe, z, at_x), device(pipe, z, at_y)
    z_dev = [device(pipe, flip(z, k), xy) for k in range(4)]
    back_dev = [device(1 - pipe, flip(z, k), xy) for k in range(4)]

    barrier = pltpu.get_barrier_semaphore()
    for other in [x_dev, y_dev] + z_dev[1:] + back_dev:
        pl.semaphore_signal(barrier, inc=1, device_id=other, device_id_type=MESH)

    loads = [
        pltpu.make_async_copy(x_hbm, x_v, load_sem.at[0]),
        pltpu.make_async_copy(g_hbm, g_v, load_sem.at[1]),
        pltpu.make_async_copy(wg_hbm, wgu.at[:, :, pl.ds(0, block)], load_sem.at[2]),
        pltpu.make_async_copy(wu_hbm, wgu.at[:, :, pl.ds(block, block)], load_sem.at[3]),
        pltpu.make_async_copy(wd_hbm, wd_v, load_sem.at[4]),
    ]
    for copy in loads:
        copy.start()

    tok = route_ref.shape[1]
    hit = route_ref[...] == 0
    member = jnp.sum(jnp.where(hit, 1.0, 0.0), axis=0, keepdims=True)
    weight = jnp.sum(jnp.where(hit, gate_ref[...], 0.0), axis=0, keepdims=True)
    earlier = lax.broadcasted_iota(jnp.int32, (tok, tok), 0) < lax.broadcasted_iota(
        jnp.int32, (tok, tok), 1
    )
    member8 = jnp.broadcast_to(member, (8, tok))
    position = jnp.dot(
        member8.astype(jnp.bfloat16),
        jnp.where(earlier, 1.0, 0.0).astype(jnp.bfloat16),
        preferred_element_type=jnp.float32,
    )
    slot = lax.broadcasted_iota(jnp.int32, (8, tok), 0).astype(jnp.float32)
    pick = jnp.where((member8 == 1.0) & (position == slot), 1.0, 0.0)
    coef = jnp.sum(pick * weight, axis=1, keepdims=True)
    pick_mat = pick.astype(jnp.bfloat16)

    for kind in range(2):
        loads[kind].wait()
        source = x_v if kind == 0 else g_v
        for q in range(PIECES):
            rows = jnp.dot(
                pick_mat, source[:, q * piece:(q + 1) * piece], preferred_element_type=jnp.float32
            )
            scaled = rows if kind == 0 else rows * coef
            for i in range(slots):
                staged[i, kind * PIECES + q:kind * PIECES + q + 1, :] = scaled[i:i + 1, :]
                if kind == 1:
                    plain[i, q:q + 1, :] = rows[i:i + 1, :]
    own = xy * 4 + z
    for i in range(slots):
        gath[own, i] = staged[i].astype(jnp.bfloat16)
    plain_in[0] = plain[...].astype(jnp.bfloat16)

    pl.semaphore_wait(barrier, 9)

    def remote(src, dst, send, recv, to):
        return pltpu.make_async_remote_copy(
            src_ref=src, dst_ref=dst, send_sem=send, recv_sem=recv, device_id=to,
            device_id_type=MESH,
        )

    def halves(k):
        cut = 3 if k % 2 == 0 else 2
        return (pl.ds(0, cut), pl.ds(cut, slots - cut))

    sent = []

    def start(copy):
        copy.start()
        sent.append(copy)
        return copy

    arrivals_z = {}
    for k in (1, 3, 2):
        arrivals_z[k] = start(
            remote(gath.at[own], gath.at[own], z_send.at[k], z_recv.at[k], z_dev[k])
        )

    def slab(spot, k, half):
        return gath.at[spot * 4 + flip(z, k), halves(k)[half]]

    def to_plane(k):
        for half in range(2):
            start(remote(slab(xy, k, half), slab(xy, k, half), xy_send.at[0, k, half],
                         xy_recv.at[0, k, half], x_dev))
            start(remote(slab(xy, k, 1 - half), slab(xy, k, 1 - half),
                         xy_send.at[1, k, 1 - half], xy_recv.at[1, k, 1 - half], y_dev))

    def arrived(axis, k, half):
        spot = at_x if axis == 0 else at_y
        remote(slab(spot, k, half), slab(spot, k, half), xy_send.at[axis, k, half],
               xy_recv.at[axis, k, half], x_dev).wait_recv()

    def to_corner(k):
        arrived(0, k, 0)
        start(remote(slab(at_x, k, 0), slab(at_x, k, 0), d_send.at[k, 0], d_recv.at[k, 0], y_dev))
        arrived(1, k, 1)
        start(remote(slab(at_y, k, 1), slab(at_y, k, 1), d_send.at[k, 1], d_recv.at[k, 1], x_dev))

    to_plane(0)
    plain_copy = start(
        remote(plain_in.at[0], plain_in.at[1], p_send, p_recv, back_dev[0])
    )
    before = 0
    for k in (1, 3, 2):
        spot = gath.at[xy * 4 + flip(z, k)]
        remote(spot, spot, z_send.at[k], z_recv.at[k], z_dev[k]).wait_recv()
        to_plane(k)
        to_corner(before)
        before = k
    to_corner(before)
    for copy in loads[2:]:
        copy.wait()
    for k in (0, 1, 3, 2):
        arrived(0, k, 1)
        arrived(1, k, 0)
        for half in range(2):
            remote(slab(at_d, k, half), slab(at_d, k, half), d_send.at[k, half],
                   d_recv.at[k, half], y_dev).wait_recv()

    for i in range(slots):
        packed = gath[:, i].reshape(SHARDS * 2 * PIECES, piece)
        ordered = jnp.dot(
            perm_ref[...], packed, preferred_element_type=jnp.float32
        ).astype(jnp.bfloat16)
        for q in range(PIECES):
            xf[q, i * SHARDS:(i + 1) * SHARDS, :] = ordered[q * SHARDS:(q + 1) * SHARDS]
            gf[q, i * SHARDS:(i + 1) * SHARDS, :] = ordered[
                (PIECES + q) * SHARDS:(PIECES + q + 1) * SHARDS
            ]

    rows_all = slots * SHARDS
    pre = jnp.zeros((rows_all, 2 * block), jnp.float32)
    back = jnp.zeros((rows_all, block), jnp.float32)
    for q in range(PIECES):
        pre = pre + jnp.dot(xf[q], wgu[q], preferred_element_type=jnp.float32)
        back = back + lax.dot_general(
            gf[q], wd_v[:, q * piece:(q + 1) * piece], CONTRACT_LAST,
            preferred_element_type=jnp.float32,
        )
    hidden, grad_gate, grad_up = hidden_grads(pre[:, :block], pre[:, block:], back)
    grad_both = jnp.concatenate(
        [grad_gate.astype(jnp.bfloat16), grad_up.astype(jnp.bfloat16)], axis=1
    )
    for q in range(PIECES):
        share = lax.dot_general(
            grad_both, wgu[q], CONTRACT_LAST, preferred_element_type=jnp.float32
        ).astype(jnp.bfloat16)
        for i in range(slots):
            pfull[i, q * SHARDS:(q + 1) * SHARDS, :] = share[i * SHARDS:(i + 1) * SHARDS]

    low, high = pl.ds(0, 2), pl.ds(2, 2)
    for i in range(slots):
        units = jnp.dot(
            unperm_ref[...], pfull[i], preferred_element_type=jnp.float32
        ).astype(jnp.bfloat16)
        part[i] = units.reshape(4, 4, PIECES, piece)
        start(remote(part.at[i, at_d, low], diag_in.at[i, low], s1_send.at[i, 0],
                     s1_recv.at[i, 0], y_dev))
        start(remote(part.at[i, at_d, high], diag_in.at[i, high], s1_send.at[i, 1],
                     s1_recv.at[i, 1], x_dev))
    for i in range(slots):
        start(remote(part.at[i, at_x, high], in_x.at[i, high], s1_send.at[i, 2],
                     s1_recv.at[i, 2], x_dev))
        start(remote(part.at[i, at_y, low], in_y.at[i, low], s1_send.at[i, 3],
                     s1_recv.at[i, 3], y_dev))

    hidden_t = jnp.transpose(hidden).astype(jnp.bfloat16)

    def down_piece(q):
        down_v[:, q * piece:(q + 1) * piece] = jnp.dot(
            hidden_t, gf[q], preferred_element_type=jnp.float32
        ).astype(jnp.bfloat16)

    for q in range(PIECES // 2):
        down_piece(q)

    for i in range(slots):
        remote(part.at[i, at_d, low], diag_in.at[i, low], s1_send.at[i, 0],
               s1_recv.at[i, 0], y_dev).wait_recv()
        fwd_x[i] = (
            part[i, at_x, low].astype(jnp.float32) + diag_in[i, low].astype(jnp.float32)
        ).astype(jnp.bfloat16)
        start(remote(fwd_x.at[i], in_x.at[i, low], s2_send.at[i, 0], s2_recv.at[i, 0], x_dev))
        remote(part.at[i, at_d, high], diag_in.at[i, high], s1_send.at[i, 1],
               s1_recv.at[i, 1], x_dev).wait_recv()
        fwd_y[i] = (
            part[i, at_y, high].astype(jnp.float32) + diag_in[i, high].astype(jnp.float32)
        ).astype(jnp.bfloat16)
        start(remote(fwd_y.at[i], in_y.at[i, high], s2_send.at[i, 1], s2_recv.at[i, 1], y_dev))

    for q in range(PIECES // 2, PIECES):
        down_piece(q)
    down_copy = pltpu.make_async_copy(down_v, down_out, out_sem.at[0])
    down_copy.start()

    for i in range(slots):
        remote(part.at[i, at_x, high], in_x.at[i, high], s1_send.at[i, 2],
               s1_recv.at[i, 2], x_dev).wait_recv()
        remote(part.at[i, at_y, low], in_y.at[i, low], s1_send.at[i, 3],
               s1_recv.at[i, 3], y_dev).wait_recv()
        remote(fwd_x.at[i], in_x.at[i, low], s2_send.at[i, 0], s2_recv.at[i, 0],
               x_dev).wait_recv()
        remote(fwd_y.at[i], in_y.at[i, high], s2_send.at[i, 1], s2_recv.at[i, 1],
               y_dev).wait_recv()
        zsum[i] = (
            part[i, xy].astype(jnp.float32) + in_x[i].astype(jnp.float32)
            + in_y[i].astype(jnp.float32)
        ).astype(jnp.bfloat16)
        for k in (2, 3, 1, 0):
            start(remote(zsum.at[i, flip(z, k)], in_z.at[i, z], s3_send.at[i, k],
                         s3_recv.at[i, k], back_dev[k]))

    plain_copy.wait_recv()
    for i in range(slots):
        total = plain_in[1, i].astype(jnp.float32)
        for k in range(4):
            remote(zsum.at[i, 0], in_z.at[i, flip(z, k)], s3_send.at[i, k],
                   s3_recv.at[i, k], back_dev[k]).wait_recv()
        for zz in range(4):
            total = total + in_z[i, zz].astype(jnp.float32)
        rows_v[i] = total
    rows_copy = pltpu.make_async_copy(rows_v, rows_out, out_sem.at[1])
    rows_copy.start()
    for copy in sent:
        copy.wait_send()
    down_copy.wait()
    rows_copy.wait()


def group_work(inputs, grads, gate_cols, up_cols, down_rows, route, gate):
    tok, width = inputs.shape
    block = gate_cols.shape[1]
    piece = width // PIECES
    bf16 = jnp.bfloat16
    wide = SHARDS * 2 * PIECES
    r, c = lax.broadcasted_iota(jnp.int32, (wide, wide), 0), lax.broadcasted_iota(
        jnp.int32, (wide, wide), 1
    )
    perm = ((r % SHARDS == c // (2 * PIECES)) & (r // SHARDS == c % (2 * PIECES))).astype(bf16)
    half = SHARDS * PIECES
    r, c = r[:half, :half], c[:half, :half]
    unperm = ((r // PIECES == c % SHARDS) & (r % PIECES == c // SHARDS)).astype(bf16)
    whole = pl.BlockSpec(memory_space=pl.ANY)
    vmem = pl.BlockSpec(memory_space=pltpu.VMEM)
    dma = pltpu.SemaphoreType.DMA
    units = pltpu.VMEM((CAP, 4, PIECES, piece), bf16)
    rows, down = pl.pallas_call(
        group_kernel,
        out_shape=(
            jax.ShapeDtypeStruct((CAP, PIECES, piece), jnp.float32),
            jax.ShapeDtypeStruct((block, width), bf16),
        ),
        in_specs=[whole] * 5 + [vmem] * 4,
        out_specs=(whole, whole),
        scratch_shapes=[
            pltpu.VMEM((tok, width), bf16),
            pltpu.VMEM((tok, width), bf16),
            pltpu.VMEM((PIECES, piece, 2 * block), bf16),
            pltpu.VMEM((block, width), bf16),
            pltpu.VMEM((CAP, 2 * PIECES, piece), jnp.float32),
            pltpu.VMEM((CAP, PIECES, piece), jnp.float32),
            pltpu.VMEM((2, CAP, PIECES, piece), bf16),
            pltpu.VMEM((SHARDS, CAP, 2 * PIECES, piece), bf16),
            pltpu.VMEM((PIECES, CAP * SHARDS, piece), bf16),
            pltpu.VMEM((PIECES, CAP * SHARDS, piece), bf16),
            pltpu.VMEM((CAP, half, piece), bf16),
            pltpu.VMEM((CAP, 4, 4, PIECES, piece), bf16),
            units,
            pltpu.VMEM((CAP, 2, PIECES, piece), bf16),
            pltpu.VMEM((CAP, 2, PIECES, piece), bf16),
            units,
            units,
            units,
            units,
            pltpu.VMEM((block, width), bf16),
            pltpu.VMEM((CAP, PIECES, piece), jnp.float32),
            dma((5,)), dma((2,)), dma((4,)), dma((4,)), dma((2, 4, 2)), dma((2, 4, 2)),
            dma((4, 2)), dma((4, 2)), dma, dma,
            dma((CAP, 4)), dma((CAP, 4)), dma((CAP, 2)), dma((CAP, 2)),
            dma((CAP, 4)), dma((CAP, 4)),
        ],
        compiler_params=pltpu.CompilerParams(
            collective_id=0, has_side_effects=True, vmem_limit_bytes=48 * 2**20
        ),
        cost_estimate=pl.CostEstimate(
            flops=12 * CAP * SHARDS * width * block, bytes_accessed=14 * tok * width,
            transcendentals=CAP * SHARDS * block,
        ),
        name="relay_group",
    )(
        inputs, grads, gate_cols.reshape(PIECES, piece, block),
        up_cols.reshape(PIECES, piece, block), down_rows, route.T, gate.T, perm, unperm,
    )
    return rows.reshape(CAP, width), down


def plain_work(rows, gate_cols, up_cols, down_rows):
    width = lax.axis_size("expert")
    live = width // SHARDS
    across = [[g * SHARDS + j for g in range(live)] for j in range(SHARDS)]
    within = [[g * SHARDS + j for j in range(SHARDS)] for g in range(live)]
    kinds, count, model_width = rows.shape
    if live > 1:
        rows = lax.all_to_all(
            rows, "expert", split_axis=1, concat_axis=1, tiled=True, axis_index_groups=across
        )
    got = lax.all_gather(rows, "expert", axis=1, tiled=True, axis_index_groups=within)
    flat_in, flat_grad = got[0], got[1]
    gate_pre = jnp.dot(flat_in, gate_cols, preferred_element_type=jnp.float32)
    up_pre = jnp.dot(flat_in, up_cols, preferred_element_type=jnp.float32)
    back = lax.dot_general(flat_grad, down_rows, CONTRACT_LAST, preferred_element_type=jnp.float32)
    hidden, grad_gate, grad_up = hidden_grads(gate_pre, up_pre, back)
    share = lax.dot_general(
        grad_gate.astype(jnp.bfloat16), gate_cols, CONTRACT_LAST,
        preferred_element_type=jnp.float32,
    ) + lax.dot_general(
        grad_up.astype(jnp.bfloat16), up_cols, CONTRACT_LAST, preferred_element_type=jnp.float32
    )
    summed = lax.psum_scatter(
        share.astype(jnp.bfloat16), "expert", scatter_dimension=0, tiled=True,
        axis_index_groups=within,
    )
    if live > 1:
        summed = lax.all_to_all(
            summed, "expert", split_axis=0, concat_axis=0, tiled=True, axis_index_groups=across
        )
    down_part = lax.dot_general(
        hidden.astype(jnp.bfloat16), flat_grad, ROWS_FIRST, preferred_element_type=jnp.float32
    ).astype(jnp.bfloat16)
    return summed, down_part


def slot_picks(route, gate, live):
    hit = route[:, :, None] == jnp.arange(live, dtype=jnp.int32)
    member = jnp.sum(hit.astype(jnp.int32), axis=1)
    weight = jnp.sum(jnp.where(hit, gate[:, :, None], 0.0), axis=1)
    position = jnp.cumsum(member, axis=0) - member
    pick = (member[:, :, None] == 1) & (
        position[:, :, None] == jnp.arange(CAP, dtype=jnp.int32)
    )
    return member, weight, pick


def other_core(value):
    return lax.ppermute(value, "pipe", [(0, 1), (1, 0)])


def body(section_inputs, output_grads, w_gate, w_up, w_down, route_ids, route_gates):
    inputs, grads, route, gate = section_inputs[0], output_grads[0], route_ids[0], route_gates[0]
    gate_cols, up_cols, down_rows = w_gate[0], w_up[0], w_down[0]
    tok_rows = inputs.shape[0]
    live = lax.axis_size("expert") // SHARDS
    if live == 1:
        grads_behind = other_core(grads)
        route_behind = other_core(route)
        rows, down_part = group_work(inputs, grads, gate_cols, up_cols, down_rows, route, gate)
        member, _, pick = slot_picks(route_behind, gate, 1)
        placed = jnp.dot(
            pick.reshape(tok_rows, CAP).astype(jnp.bfloat16), rows.astype(jnp.bfloat16),
            preferred_element_type=jnp.float32,
        )
        handed = jnp.where(member == 1, placed.astype(jnp.bfloat16), grads_behind)
        return handed[None], down_part[None]
    _, weight, pick = slot_picks(route, gate, live)
    pick_mat = pick.astype(jnp.bfloat16).reshape(tok_rows, live * CAP)
    rows_in = lax.dot_general(pick_mat, inputs, ROWS_FIRST, preferred_element_type=jnp.float32)
    chosen = lax.dot_general(pick_mat, grads, ROWS_FIRST, preferred_element_type=jnp.float32)
    slot_gate = jnp.sum(pick.astype(jnp.float32) * weight[:, :, None], axis=0).reshape(-1, 1)
    rows = jnp.stack([rows_in.astype(jnp.bfloat16), (chosen * slot_gate).astype(jnp.bfloat16)])
    summed, down_part = plain_work(rows, gate_cols, up_cols, down_rows)
    branch = jnp.dot(pick_mat, summed, preferred_element_type=jnp.float32)
    input_grad = (grads.astype(jnp.float32) + branch).astype(jnp.bfloat16)
    return other_core(input_grad)[None], down_part[None]


def solution(mesh):
    return jax.shard_map(
        body,
        mesh=mesh,
        in_specs=(
            P("pipe", "expert", None),
            P("pipe", "expert", None),
            P("pipe", None, "expert"),
            P("pipe", None, "expert"),
            P("pipe", "expert", None),
            P("pipe", "expert", None),
            P("pipe", "expert", None),
        ),
        out_specs=(P("pipe", "expert", None), P("pipe", "expert", None)),
        check_vma=False,
    )
```

time: 169 us -> 58.8 us (0.35)
  the two profiles are of different devices: /device:TPU:13 before, /device:TPU:1 now
where the time goes in v1:
time: 58.8 us; the launch traced here: 58.6 us
  Pallas kernels  47.1 us (80%)
  local copies, waits for them, and re-layouts  5.73 us (10%)
  matrix products  3.55 us (6%)
  other arithmetic  0.82 us (1%)
  between operations  0.75 us (1%)
    pallas_call x1, Pallas kernels, group_work(): pl.pallas_call(group_kernel, out_shape=(jax.ShapeDtypeStruct((CAP, PIECES...  47.1 us
    unnamed x10, local copies, waits for them, and re-layouts  5.61 us
    dot_general x1, matrix products, body(): jnp.dot(pick.reshape(tok_rows, CAP).astype(jnp.bfloat16), rows.astype(jnp...  3.55 us
  transfers between devices with their start and end apart: 2, of which 0 were waited for; matrix products, arithmetic and copies ran while one was open for 2% of the time, Pallas kernels for 80%

profile of v1, /device:TPU:1, one launch (start us, length us, event | category | flops | bytes accessed | tf_op | source)
XLA Modules:
  0.0 58.6 jit_solution(12894860646313565281)
XLA Ops:
  0.6 0.1 collective-permute-start
  0.8 0.5 collective-permute-start.1
  1.3 0.2 fusion.3.unperm_ref
  1.5 0.3 fusion.1.perm_ref
  1.8 0.0 copy-start
  1.8 1.5 %copy-done = bf16[1,128,7168]{2,1,0:T(8,128)(2,1)S(1)} copy-done((bf16[1,128,7168]{2,1,0:T(8,128)(2,1)S(1)}, bf16[1,128,7168]{2,1,0:T(8,128)(2,1)}, u32[]{:S(2)}) %copy-start) | copy-done | bytes 1835032
  3.3 0.0 copy-start.1
  3.3 1.5 %copy-done.1 = bf16[1,128,7168]{2,1,0:T(8,128)(2,1)S(1)} copy-done((bf16[1,128,7168]{2,1,0:T(8,128)(2,1)S(1)}, bf16[1,128,7168]{2,1,0:T(8,128)(2,1)}, u32[]{:S(2)}) %copy-start.1) | copy-done | bytes 1835032
  4.8 0.0 copy-start.2
  4.8 0.7 %copy-done.2 = f32[1,128,8]{1,2,0:T(8,128)S(1)} copy-done((f32[1,128,8]{1,2,0:T(8,128)S(1)}, f32[1,128,8]{1,2,0:T(8,128)}, u32[]{:S(2)}) %copy-start.2) | copy-done | bytes 4120
  5.4 0.0 copy-start.3
  5.4 0.7 %copy-done.3 = s32[1,128,8]{1,2,0:T(8,128)S(1)} copy-done((s32[1,128,8]{1,2,0:T(8,128)S(1)}, s32[1,128,8]{1,2,0:T(8,128)}, u32[]{:S(2)}) %copy-start.3) | copy-done | bytes 4120
  6.1 47.1 %relay_group.1 = (f32[5,8,896]{2,1,0:T(8,128)S(1)}, bf16[128,7168]{1,0:T(8,128)(2,1)S(1)}) custom-call(bf16[128,7168]{1,0:T(8,128)(2,1)S(1)} %bitcast.25, bf16[128,7168]{1,0:T(8,128)(2,1)S(1)} %bitcast.27, bf16[8,896,128]{2,1,0:T(8,128)(2,1)} %bitcast.31, bf16[8,896,128]{2,1,0:T(8,128)(2,1)} %bitcast.32, bf16[128,7168]{1,0:T(8,128)(2,1)} %bitcast.33, ...), custom_call_target="tpu_custom_call" | custom-call | flops 880803840 | bytes 12845056 | tf_op jit(solution)/shard_map/relay_group/pallas_call | solution.py:304
  53.3 0.0 collective-permute-done
  53.4 0.1 copy.10
  53.5 0.2 reduce-window.7
  53.6 0.1 reduce.2
  53.8 0.0 collective-permute-done.1
  53.8 3.6 %select_bitcast_fusion = bf16[1,128,7168]{2,1,0:T(8,128)(2,1)} fusion(bf16[128,7168]{1,0:T(8,128)(2,1)} %collective-permute-done.1, pred[128]{0:T(512)(128)(4,1)S(1)} %broadcast_compare_fusion.1, bf16[5,7168]{1,0:T(8,128)(2,1)S(1)} %bitcast.34, s32[128]{0:T(128)S(1)} %sub.31), kind=kOutput, calls=%fused_computation.1 | convolution fusion | flops 11011328 | bytes 3742336 | tf_op jit(solution)/shard_map/dot_general | solution.py:415
  57.3 1.2 %copy.13 = bf16[1,128,7168]{2,1,0:T(8,128)(2,1)} copy(bf16[1,128,7168]{2,1,0:T(8,128)(2,1)S(1)} %bitcast.24) | data formatting | bytes 3670016
  (14 shorter events, 0.1 us)
Async XLA Ops:
  0.6 52.7 %collective-permute-start = (s32[128,8]{0,1:T(8,128)}, s32[128,8]{0,1:T(8,128)S(1)}, u32[]{:S(2)}, u32[]{:S(2)}) collective-permute-start(s32[128,8]{0,1:T(8,128)} %bitcast.29), channel_id=1, source_target_pairs={{0,16},{16,0},{1,17},{17,1},{2,18},{18,2},{3,19},{19,3},{4,20},{20... | collective-permute-start | bytes 12296 | tf_op jit(solution)/shard_map/ppermute | solution.py:402
  0.8 53.0 %collective-permute-start.1 = (bf16[128,7168]{1,0:T(8,128)(2,1)}, bf16[128,7168]{1,0:T(8,128)(2,1)}, u32[]{:S(2)}, u32[]{:S(2)}) collective-permute-start(bf16[128,7168]{1,0:T(8,128)(2,1)} %bitcast.26), channel_id=1, source_target_pairs={{0,16},{16,0},{1,17},{17,1},{2,18},{18,2},{3,19},{19,3},{4,20},{20... | collective-permute-start | bytes 5505032 | tf_op jit(solution)/shard_map/ppermute | solution.py:402
  1.8 1.5 %copy-start = (bf16[1,128,7168]{2,1,0:T(8,128)(2,1)S(1)}, bf16[1,128,7168]{2,1,0:T(8,128)(2,1)}, u32[]{:S(2)}) copy-start(bf16[1,128,7168]{2,1,0:T(8,128)(2,1)} %param.7) | copy-start | bytes 5505028
  3.3 1.5 %copy-start.1 = (bf16[1,128,7168]{2,1,0:T(8,128)(2,1)S(1)}, bf16[1,128,7168]{2,1,0:T(8,128)(2,1)}, u32[]{:S(2)}) copy-start(bf16[1,128,7168]{2,1,0:T(8,128)(2,1)} %param.8) | copy-start | bytes 5505028
  4.8 0.7 %copy-start.2 = (f32[1,128,8]{1,2,0:T(8,128)S(1)}, f32[1,128,8]{1,2,0:T(8,128)}, u32[]{:S(2)}) copy-start(f32[1,128,8]{1,2,0:T(8,128)} %param.13) | copy-start | bytes 12292
  5.4 0.7 %copy-start.3 = (s32[1,128,8]{1,2,0:T(8,128)S(1)}, s32[1,128,8]{1,2,0:T(8,128)}, u32[]{:S(2)}) copy-start(s32[1,128,8]{1,2,0:T(8,128)} %param.12) | copy-start | bytes 12292

commit v2 on v1

v2 whole, which is shorter than its diff:
```python
import jax
import jax.numpy as jnp
from jax import lax
from jax.experimental import pallas as pl
from jax.experimental.pallas import tpu as pltpu
from jax.sharding import PartitionSpec as P

SHARDS = 16
CAP = 5
PIECES = 8
MESH = pl.DeviceIdType.MESH
CONTRACT_LAST = (((1,), (1,)), ((), ()))
ROWS_FIRST = (((0,), (0,)), ((), ()))


def hidden_grads(gate_pre, up_pre, back_hidden):
    sigma = jax.nn.sigmoid(gate_pre)
    silu_gate = gate_pre * sigma
    hidden = silu_gate * up_pre
    grad_gate = back_hidden * up_pre * sigma * (1.0 + gate_pre * (1.0 - sigma))
    grad_up = back_hidden * silu_gate
    return hidden, grad_gate, grad_up


def flip(z, k):
    if k == 0:
        return z
    if k == 1:
        return z + 1 - 2 * lax.rem(z, 2)
    if k == 2:
        return lax.rem(z + 2, 4)
    return 3 - z


def pick_slots(route, gate):
    tok = route.shape[1]
    hit = route == 0
    member = jnp.sum(jnp.where(hit, 1.0, 0.0), axis=0, keepdims=True)
    earlier = lax.broadcasted_iota(jnp.int32, (tok, tok), 0) < lax.broadcasted_iota(
        jnp.int32, (tok, tok), 1
    )
    member8 = jnp.broadcast_to(member, (8, tok))
    position = jnp.dot(
        member8.astype(jnp.bfloat16),
        jnp.where(earlier, 1.0, 0.0).astype(jnp.bfloat16),
        preferred_element_type=jnp.float32,
    )
    slot = lax.broadcasted_iota(jnp.int32, (8, tok), 0).astype(jnp.float32)
    pick = jnp.where((member8 == 1.0) & (position == slot), 1.0, 0.0)
    if gate is None:
        return pick, None
    weight = jnp.sum(jnp.where(hit, gate, 0.0), axis=0, keepdims=True)
    return pick, jnp.sum(pick * weight, axis=1, keepdims=True)


def swap_order(outer, inner):
    size = outer * inner
    r = lax.broadcasted_iota(jnp.int32, (size, size), 0)
    c = lax.broadcasted_iota(jnp.int32, (size, size), 1)
    source = lax.rem(r, outer) * inner + r // outer
    return jnp.where(c == source, 1.0, 0.0).astype(jnp.bfloat16)


def group_kernel(
    x_hbm, g_hbm, wg_hbm, wu_hbm, wd_hbm, route_hbm, gate_hbm,
    rows_out, down_out,
    route_v, gate_v, x_v, g_v, wgu, wd_v, staged, plain, plain_in, gath, xf, gf, pfull, part,
    diag_in, fwd_x, fwd_y, in_x, in_y, zsum, in_z, down_v, rows_v,
    load_sem, out_sem, z_send, z_recv, xy_send, xy_recv, d_send, d_recv, dz_send, dz_recv,
    p_send, p_recv, s1_send, s1_recv, s2_send, s2_recv, s3_send, s3_recv,
):
    slots, piece = staged.shape[0], staged.shape[2]
    block = wd_v.shape[0]
    pipe = lax.axis_index("pipe")
    me = lax.axis_index("expert")
    base = (me // SHARDS) * SHARDS
    local = lax.rem(me, SHARDS)
    z = local // 4
    xy = lax.rem(local, 4)
    y, x = xy // 2, lax.rem(xy, 2)
    at_x, at_y, at_d = y * 2 + 1 - x, (1 - y) * 2 + x, 3 - xy

    def device(p, zz, spot):
        return {"pipe": p, "expert": base + zz * 4 + spot}

    x_dev, y_dev = device(pipe, z, at_x), device(pipe, z, at_y)
    z_dev = [device(pipe, flip(z, k), xy) for k in range(4)]
    back_dev = [device(1 - pipe, flip(z, k), xy) for k in range(4)]

    barrier = pltpu.get_barrier_semaphore()
    for other in [x_dev, y_dev] + z_dev[1:] + back_dev:
        pl.semaphore_signal(barrier, inc=1, device_id=other, device_id_type=MESH)

    def cols(q):
        return pl.ds(q * piece, piece)

    small = [
        pltpu.make_async_copy(route_hbm, route_v, load_sem.at[0]),
        pltpu.make_async_copy(gate_hbm, gate_v, load_sem.at[1]),
    ]
    row_loads = [
        [
            pltpu.make_async_copy(src.at[:, cols(q)], dst.at[:, cols(q)],
                                  load_sem.at[5 + kind * PIECES + q])
            for q in range(PIECES)
        ]
        for kind, (src, dst) in enumerate(((x_hbm, x_v), (g_hbm, g_v)))
    ]
    weights = [
        pltpu.make_async_copy(wg_hbm, wgu.at[:, :, pl.ds(0, block)], load_sem.at[2]),
        pltpu.make_async_copy(wu_hbm, wgu.at[:, :, pl.ds(block, block)], load_sem.at[3]),
        pltpu.make_async_copy(wd_hbm, wd_v, load_sem.at[4]),
    ]
    for copy in small + row_loads[0] + row_loads[1]:
        copy.start()
    for copy in small:
        copy.wait()
    pick, coef = pick_slots(route_v[...], gate_v[...])
    pick_mat = pick.astype(jnp.bfloat16)

    for kind in range(2):
        source = x_v if kind == 0 else g_v
        for q in range(PIECES):
            row_loads[kind][q].wait()
            rows = jnp.dot(
                pick_mat, source[:, q * piece:(q + 1) * piece], preferred_element_type=jnp.float32
            )
            scaled = rows if kind == 0 else rows * coef
            for i in range(slots):
                staged[i, kind * PIECES + q:kind * PIECES + q + 1, :] = scaled[i:i + 1, :]
                if kind == 1:
                    plain[i, q:q + 1, :] = rows[i:i + 1, :]

    def index(spot, k):
        return (k % 2) * 8 + spot * 2 + lax.rem(z // 2 + k // 2, 2)

    own = index(xy, 0)
    for i in range(slots):
        gath[own, i] = staged[i].astype(jnp.bfloat16)
    plain_in[0] = plain[...].astype(jnp.bfloat16)
    for copy in weights:
        copy.start()
    pl.semaphore_wait(barrier, 9)

    def remote(src, dst, send, recv, to):
        return pltpu.make_async_remote_copy(
            src_ref=src, dst_ref=dst, send_sem=send, recv_sem=recv, device_id=to,
            device_id_type=MESH,
        )

    sent = []

    def start(copy):
        copy.start()
        sent.append(copy)
        return copy

    for k in (2, 1, 3):
        start(remote(gath.at[own], gath.at[(k % 2) * 8 + xy * 2 + z // 2],
                     z_send.at[k], z_recv.at[k], z_dev[k]))

    def halves(k):
        if k % 2 == 1:
            return (pl.ds(0, slots),)
        cut = 3 if k == 0 else 2
        return (pl.ds(0, cut), pl.ds(cut, slots - cut))

    def slab(spot, k, half):
        return gath.at[index(spot, k), halves(k)[half]]

    def over(axis, k, half):
        ref = slab(xy, k, half)
        return remote(ref, ref, xy_send.at[axis, k, half], xy_recv.at[axis, k, half],
                      x_dev if axis == 0 else y_dev)

    def to_plane(k):
        if k % 2 == 1:
            start(over(0, k, 0))
            start(over(1, k, 0))
        else:
            start(over(0, k, 0))
            start(over(1, k, 1))
            start(over(0, k, 1))
            start(over(1, k, 0))

    def arrived(axis, k, half):
        ref = slab(at_x if axis == 0 else at_y, k, half)
        remote(ref, ref, xy_send.at[axis, k, half], xy_recv.at[axis, k, half], x_dev).wait_recv()

    def to_corner(k):
        arrived(0, k, 0)
        ref = slab(at_x, k, 0)
        start(remote(ref, ref, d_send.at[k // 2, 0], d_recv.at[k // 2, 0], y_dev))
        arrived(1, k, 1)
        ref = slab(at_y, k, 1)
        start(remote(ref, ref, d_send.at[k // 2, 1], d_recv.at[k // 2, 1], x_dev))

    def corner_arrived(k):
        for half in range(2):
            ref = slab(at_d, k, half)
            remote(ref, ref, d_send.at[k // 2, half], d_recv.at[k // 2, half], y_dev).wait_recv()

    def z_arrived(k):
        ref = gath.at[index(xy, k)]
        remote(ref, ref, z_send.at[k], z_recv.at[k], z_dev[k]).wait_recv()

    def corner_over_z(k):
        source = index(at_d, k)
        return remote(gath.at[source], gath.at[8 + source], dz_send.at[k // 2],
                      dz_recv.at[k // 2], z_dev[1])

    to_plane(0)
    plain_copy = start(remote(plain_in.at[0], plain_in.at[1], p_send, p_recv, back_dev[0]))
    z_arrived(2)
    to_plane(2)
    to_corner(0)
    to_corner(2)
    z_arrived(1)
    to_plane(1)
    corner_arrived(0)
    start(corner_over_z(0))
    z_arrived(3)
    to_plane(3)
    corner_arrived(2)
    start(corner_over_z(2))

    group_rows = slots * 8
    to_rows = swap_order(8, 2 * PIECES)
    to_units = swap_order(PIECES, 8)
    chunks = ((0, 3), (3, slots - 3))

    def compute(r):
        for i in range(slots):
            packed = gath[r * 8:(r + 1) * 8, i].reshape(8 * 2 * PIECES, piece)
            ordered = jnp.dot(to_rows, packed, preferred_element_type=jnp.float32)
            at = r * group_rows + i * 8
            for q in range(PIECES):
                xf[q, at:at + 8, :] = ordered[q * 8:(q + 1) * 8].astype(jnp.bfloat16)
                gf[q, at:at + 8, :] = ordered[
                    (PIECES + q) * 8:(PIECES + q + 1) * 8
                ].astype(jnp.bfloat16)
        mine = slice(r * group_rows, (r + 1) * group_rows)
        pre = jnp.zeros((group_rows, 2 * block), jnp.float32)
        back = jnp.zeros((group_rows, block), jnp.float32)
        for q in range(PIECES):
            pre = pre + jnp.dot(xf[q, mine, :], wgu[q], preferred_element_type=jnp.float32)
            back = back + lax.dot_general(
                gf[q, mine, :], wd_v[:, q * piece:(q + 1) * piece], CONTRACT_LAST,
                preferred_element_type=jnp.float32,
            )
        hidden, grad_gate, grad_up = hidden_grads(pre[:, :block], pre[:, block:], back)
        grad_both = jnp.concatenate(
            [grad_gate.astype(jnp.bfloat16), grad_up.astype(jnp.bfloat16)], axis=1
        )
        return hidden, grad_both

    def diagonal(r, c, half):
        lo, count = chunks[c]
        at = pl.ds(lo, count)
        return remote(part.at[r, at, at_d, half], diag_in.at[r, at, half],
                      s1_send.at[r, c, half], s1_recv.at[r, c, half],
                      y_dev if half == 0 else x_dev)

    def direct(r, c, half):
        lo, count = chunks[c]
        at = pl.ds(lo, count)
        if half == 1:
            return remote(part.at[r, at, at_x, 1], in_x.at[r, at, 1], s1_send.at[r, c, 2],
                          s1_recv.at[r, c, 2], x_dev)
        return remote(part.at[r, at, at_y, 0], in_y.at[r, at, 0], s1_send.at[r, c, 3],
                      s1_recv.at[r, c, 3], y_dev)

    def passed(r, c, half):
        lo, count = chunks[c]
        at = pl.ds(lo, count)
        if half == 0:
            return remote(fwd_x.at[r, at], in_x.at[r, at, 0], s2_send.at[r, c, 0],
                          s2_recv.at[r, c, 0], x_dev)
        return remote(fwd_y.at[r, at], in_y.at[r, at, 1], s2_send.at[r, c, 1],
                      s2_recv.at[r, c, 1], y_dev)

    def homeward(r, c, k):
        lo, count = chunks[c]
        at = pl.ds(lo, count)
        return remote(zsum.at[r, at, lax.rem(z // 2 + k // 2, 2)], in_z.at[k, at],
                      s3_send.at[c, k], s3_recv.at[c, k], back_dev[k])

    def send_shares(r, grad_both):
        for q in range(PIECES):
            share = lax.dot_general(
                grad_both, wgu[q], CONTRACT_LAST, preferred_element_type=jnp.float32
            ).astype(jnp.bfloat16)
            for i in range(slots):
                pfull[r, i, q * 8:(q + 1) * 8, :] = share[i * 8:(i + 1) * 8]
        for c, (lo, count) in enumerate(chunks):
            for i in range(lo, lo + count):
                units = jnp.dot(to_units, pfull[r, i], preferred_element_type=jnp.float32)
                part[r, i] = units.reshape(4, 2, PIECES, piece).astype(jnp.bfloat16)
            for half in range(2):
                start(diagonal(r, c, half))
        for c in range(2):
            for half in range(2):
                start(direct(r, c, half))

    def pass_on(r):
        for c, (lo, count) in enumerate(chunks):
            for half in range(2):
                diagonal(r, c, half).wait_recv()
                spot, out = (at_x, fwd_x) if half == 0 else (at_y, fwd_y)
                for i in range(lo, lo + count):
                    out[r, i] = (
                        part[r, i, spot, half].astype(jnp.float32)
                        + diag_in[r, i, half].astype(jnp.float32)
                    ).astype(jnp.bfloat16)
                start(passed(r, c, half))

    def send_home(r):
        for c, (lo, count) in enumerate(chunks):
            for half in range(2):
                direct(r, c, half).wait_recv()
                passed(r, c, half).wait_recv()
            for i in range(lo, lo + count):
                zsum[r, i] = (
                    part[r, i, xy].astype(jnp.float32) + in_x[r, i].astype(jnp.float32)
                    + in_y[r, i].astype(jnp.float32)
                ).astype(jnp.bfloat16)
            for k in (r + 2, r):
                start(homeward(r, c, k))

    arrived(0, 0, 1)
    arrived(1, 0, 0)
    arrived(0, 2, 1)
    arrived(1, 2, 0)
    for copy in weights:
        copy.wait()
    hidden_a, grad_both = compute(0)
    send_shares(0, grad_both)
    for k in (1, 3):
        arrived(0, k, 0)
        arrived(1, k, 0)
    for k in (0, 2):
        corner_over_z(k).wait_recv()
    hidden_b, grad_both = compute(1)
    pass_on(0)
    send_shares(1, grad_both)
    hidden_t = jnp.transpose(jnp.concatenate([hidden_a, hidden_b], axis=0)).astype(jnp.bfloat16)

    def down_piece(q):
        down_v[:, q * piece:(q + 1) * piece] = jnp.dot(
            hidden_t, gf[q], preferred_element_type=jnp.float32
        ).astype(jnp.bfloat16)

    for q in range(PIECES // 2):
        down_piece(q)
    pass_on(1)
    send_home(0)
    for q in range(PIECES // 2, PIECES):
        down_piece(q)
    down_copy = pltpu.make_async_copy(down_v, down_out, out_sem.at[0])
    down_copy.start()
    send_home(1)

    plain_copy.wait_recv()
    rows_v[slots:] = jnp.zeros((rows_v.shape[0] - slots, rows_v.shape[1]), jnp.float32)
    for c, (lo, count) in enumerate(chunks):
        for k in range(4):
            homeward(k % 2, c, k).wait_recv()
        for i in range(lo, lo + count):
            total = plain_in[1, i].astype(jnp.float32)
            for k in range(4):
                total = total + in_z[k, i].astype(jnp.float32)
            for q in range(PIECES):
                rows_v[i:i + 1, q * piece:(q + 1) * piece] = total[q:q + 1, :]
    rows_copy = pltpu.make_async_copy(rows_v, rows_out, out_sem.at[1])
    rows_copy.start()
    for copy in sent:
        copy.wait_send()
    down_copy.wait()
    rows_copy.wait()


def group_work(inputs, grads, gate_cols, up_cols, down_rows, route, gate):
    tok, width = inputs.shape
    block = gate_cols.shape[1]
    piece = width // PIECES
    bf16 = jnp.bfloat16
    whole = pl.BlockSpec(memory_space=pl.ANY)
    dma = pltpu.SemaphoreType.DMA
    pairs = pltpu.VMEM((2, CAP, 2, PIECES, piece), bf16)
    singles = pltpu.VMEM((2, CAP, PIECES, piece), bf16)
    return pl.pallas_call(
        group_kernel,
        out_shape=(
            jax.ShapeDtypeStruct((8, width), jnp.float32),
            jax.ShapeDtypeStruct((block, width), bf16),
        ),
        in_specs=[whole] * 7,
        out_specs=(whole, whole),
        scratch_shapes=[
            pltpu.VMEM(route.shape[::-1], jnp.int32),
            pltpu.VMEM(gate.shape[::-1], jnp.float32),
            pltpu.VMEM((tok, width), bf16),
            pltpu.VMEM((tok, width), bf16),
            pltpu.VMEM((PIECES, piece, 2 * block), bf16),
            pltpu.VMEM((block, width), bf16),
            pltpu.VMEM((CAP, 2 * PIECES, piece), jnp.float32),
            pltpu.VMEM((CAP, PIECES, piece), jnp.float32),
            singles,
            pltpu.VMEM((SHARDS, CAP, 2 * PIECES, piece), bf16),
            pltpu.VMEM((PIECES, CAP * SHARDS, piece), bf16),
            pltpu.VMEM((PIECES, CAP * SHARDS, piece), bf16),
            pltpu.VMEM((2, CAP, 8 * PIECES, piece), bf16),
            pltpu.VMEM((2, CAP, 4, 2, PIECES, piece), bf16),
            pairs,
            singles,
            singles,
            pairs,
            pairs,
            pairs,
            pltpu.VMEM((4, CAP, PIECES, piece), bf16),
            pltpu.VMEM((block, width), bf16),
            pltpu.VMEM((8, width), jnp.float32),
            dma((5 + 2 * PIECES,)), dma((2,)), dma((4,)), dma((4,)), dma((2, 4, 2)),
            dma((2, 4, 2)), dma((2, 2)), dma((2, 2)), dma((2,)), dma((2,)), dma, dma,
            dma((2, 2, 4)), dma((2, 2, 4)), dma((2, 2, 2)), dma((2, 2, 2)),
            dma((2, 4)), dma((2, 4)),
        ],
        compiler_params=pltpu.CompilerParams(
            collective_id=0, has_side_effects=True, vmem_limit_bytes=60 * 2**20
        ),
        cost_estimate=pl.CostEstimate(
            flops=12 * CAP * SHARDS * width * block, bytes_accessed=14 * tok * width,
            transcendentals=CAP * SHARDS * block,
        ),
        name="relay_group",
    )(
        inputs, grads, gate_cols.reshape(PIECES, piece, block),
        up_cols.reshape(PIECES, piece, block), down_rows, route.T, gate.T,
    )


def finish_kernel(route_hbm, rows_hbm, grads_hbm, down_hbm, handed_out, down_out,
                  route_v, rows_v, grads_v, done_v, sem, down_sem):
    piece = grads_v.shape[1] // PIECES

    def cols(q):
        return pl.ds(q * piece, piece)

    first = [
        pltpu.make_async_copy(route_hbm, route_v, sem.at[0]),
        pltpu.make_async_copy(rows_hbm, rows_v, sem.at[1]),
    ]
    loads = [
        pltpu.make_async_copy(grads_hbm.at[:, cols(q)], grads_v.at[:, cols(q)], sem.at[2 + q])
        for q in range(PIECES)
    ]
    stores = [
        pltpu.make_async_copy(done_v.at[:, cols(q)], handed_out.at[:, cols(q)],
                              sem.at[2 + PIECES + q])
        for q in range(PIECES)
    ]
    downs = [
        pltpu.make_async_copy(down_hbm.at[:, cols(q)], down_out.at[:, cols(q)], down_sem.at[q])
        for q in range(PIECES)
    ]
    for copy in first + loads + downs:
        copy.start()
    for copy in first:
        copy.wait()
    pick, _ = pick_slots(route_v[...], None)
    named = jnp.transpose(pick)
    changed = jnp.sum(named, axis=1, keepdims=True) > 0.0
    named = named.astype(jnp.bfloat16)
    for q in range(PIECES):
        at = slice(q * piece, (q + 1) * piece)
        placed = jnp.dot(
            named, rows_v[:, at].astype(jnp.bfloat16), preferred_element_type=jnp.float32
        )
        loads[q].wait()
        done_v[:, at] = jnp.where(changed, placed, grads_v[:, at].astype(jnp.float32)).astype(
            jnp.bfloat16
        )
        stores[q].start()
    for copy in stores + downs:
        copy.wait()


def finish(route, rows, grads, down):
    whole = pl.BlockSpec(memory_space=pl.ANY)
    like = jax.ShapeDtypeStruct(grads.shape, grads.dtype)
    return pl.pallas_call(
        finish_kernel,
        out_shape=(like, jax.ShapeDtypeStruct(down.shape, down.dtype)),
        in_specs=[whole] * 4,
        out_specs=(whole, whole),
        scratch_shapes=[
            pltpu.VMEM(route.shape[::-1], jnp.int32),
            pltpu.VMEM(rows.shape, rows.dtype),
            pltpu.VMEM(grads.shape, grads.dtype),
            pltpu.VMEM(grads.shape, grads.dtype),
            pltpu.SemaphoreType.DMA((2 + 2 * PIECES,)),
            pltpu.SemaphoreType.DMA((PIECES,)),
        ],
        compiler_params=pltpu.CompilerParams(vmem_limit_bytes=60 * 2**20),
        cost_estimate=pl.CostEstimate(
            flops=16 * grads.size, bytes_accessed=8 * grads.size, transcendentals=0
        ),
        name="relay_finish",
    )(route.T, rows, grads, down)


def plain_work(rows, gate_cols, up_cols, down_rows):
    width = lax.axis_size("expert")
    live = width // SHARDS
    across = [[g * SHARDS + j for g in range(live)] for j in range(SHARDS)]
    within = [[g * SHARDS + j for j in range(SHARDS)] for g in range(live)]
    kinds, count, model_width = rows.shape
    if live > 1:
        rows = lax.all_to_all(
            rows, "expert", split_axis=1, concat_axis=1, tiled=True, axis_index_groups=across
        )
    got = lax.all_gather(rows, "expert", axis=1, tiled=True, axis_index_groups=within)
    flat_in, flat_grad = got[0], got[1]
    gate_pre = jnp.dot(flat_in, gate_cols, preferred_element_type=jnp.float32)
    up_pre = jnp.dot(flat_in, up_cols, preferred_element_type=jnp.float32)
    back = lax.dot_general(flat_grad, down_rows, CONTRACT_LAST, preferred_element_type=jnp.float32)
    hidden, grad_gate, grad_up = hidden_grads(gate_pre, up_pre, back)
    share = lax.dot_general(
        grad_gate.astype(jnp.bfloat16), gate_cols, CONTRACT_LAST,
        preferred_element_type=jnp.float32,
    ) + lax.dot_general(
        grad_up.astype(jnp.bfloat16), up_cols, CONTRACT_LAST, preferred_element_type=jnp.float32
    )
    summed = lax.psum_scatter(
        share.astype(jnp.bfloat16), "expert", scatter_dimension=0, tiled=True,
        axis_index_groups=within,
    )
    if live > 1:
        summed = lax.all_to_all(
            summed, "expert", split_axis=0, concat_axis=0, tiled=True, axis_index_groups=across
        )
    down_part = lax.dot_general(
        hidden.astype(jnp.bfloat16), flat_grad, ROWS_FIRST, preferred_element_type=jnp.float32
    ).astype(jnp.bfloat16)
    return summed, down_part


def slot_picks(route, gate, live):
    hit = route[:, :, None] == jnp.arange(live, dtype=jnp.int32)
    member = jnp.sum(hit.astype(jnp.int32), axis=1)
    weight = jnp.sum(jnp.where(hit, gate[:, :, None], 0.0), axis=1)
    position = jnp.cumsum(member, axis=0) - member
    pick = (member[:, :, None] == 1) & (
        position[:, :, None] == jnp.arange(CAP, dtype=jnp.int32)
    )
    return member, weight, pick


def other_core(value):
    return lax.ppermute(value, "pipe", [(0, 1), (1, 0)])


def body(section_inputs, output_grads, w_gate, w_up, w_down, route_ids, route_gates):
    inputs, grads, route, gate = section_inputs[0], output_grads[0], route_ids[0], route_gates[0]
    gate_cols, up_cols, down_rows = w_gate[0], w_up[0], w_down[0]
    tok_rows = inputs.shape[0]
    live = lax.axis_size("expert") // SHARDS
    if live == 1:
        grads_behind = other_core(grads)
        route_behind = other_core(route)
        rows, down_part = group_work(inputs, grads, gate_cols, up_cols, down_rows, route, gate)
        handed, down_part = finish(route_behind, rows, grads_behind, down_part)
        return handed[None], down_part[None]
    _, weight, pick = slot_picks(route, gate, live)
    pick_mat = pick.astype(jnp.bfloat16).reshape(tok_rows, live * CAP)
    rows_in = lax.dot_general(pick_mat, inputs, ROWS_FIRST, preferred_element_type=jnp.float32)
    chosen = lax.dot_general(pick_mat, grads, ROWS_FIRST, preferred_element_type=jnp.float32)
    slot_gate = jnp.sum(pick.astype(jnp.float32) * weight[:, :, None], axis=0).reshape(-1, 1)
    rows = jnp.stack([rows_in.astype(jnp.bfloat16), (chosen * slot_gate).astype(jnp.bfloat16)])
    summed, down_part = plain_work(rows, gate_cols, up_cols, down_rows)
    branch = jnp.dot(pick_mat, summed, preferred_element_type=jnp.float32)
    input_grad = (grads.astype(jnp.float32) + branch).astype(jnp.bfloat16)
    return other_core(input_grad)[None], down_part[None]


def solution(mesh):
    return jax.shard_map(
        body,
        mesh=mesh,
        in_specs=(
            P("pipe", "expert", None),
            P("pipe", "expert", None),
            P("pipe", None, "expert"),
            P("pipe", None, "expert"),
            P("pipe", "expert", None),
            P("pipe", "expert", None),
            P("pipe", "expert", None),
        ),
        out_specs=(P("pipe", "expert", None), P("pipe", "expert", None)),
        check_vma=False,
    )
```

time: 58.8 us -> 105 us (1.79)
  Pallas kernels: 47.1 us -> 103 us
  local copies, waits for them, and re-layouts: 5.73 us -> 1.23 us
  matrix products: 3.55 us -> 0 us
    pallas_call x1 -> x2, Pallas kernels: 47.1 us -> 103 us  [the longest x1 56.9 us: finish(): pl.pallas_call(finish_kernel, out_shape=(like, jax.ShapeDtypeStruct(down....]
    unnamed x10 -> x4, local copies, waits for them, and re-layouts: 5.61 us -> 1.23 us
    dot_general x1 -> x0, matrix products: 3.55 us -> none  [body(): jnp.dot(pick.reshape(tok_rows, CAP).astype(jnp.bfloat16), rows.astype(jnp...]
  transfers between devices with their start and end apart: 2 -> 2, of which waited for: 0 -> 0; matrix products, arithmetic and copies ran while one was open for 2% -> 0% of each run, Pallas kernels for 80% -> 44%
where the time goes in v2:
time: 105 us
  Pallas kernels  103 us (98%)
  local copies, waits for them, and re-layouts  1.23 us (1%)
    pallas_call x1, Pallas kernels, finish(): pl.pallas_call(finish_kernel, out_shape=(like, jax.ShapeDtypeStruct(down....  56.9 us
    pallas_call x1, Pallas kernels, group_work(): pl.pallas_call(group_kernel, out_shape=(jax.ShapeDtypeStruct((8, width),...  45.8 us
  transfers between devices with their start and end apart: 2, of which 0 were waited for; matrix products, arithmetic and copies ran while one was open for 0% of the time, Pallas kernels for 44%

profile of v2, /device:TPU:1, one launch (start us, length us, event | category | flops | bytes accessed | tf_op | source)
XLA Modules:
  0.0 105.2 jit_solution(13934312840445495513)
XLA Ops:
  0.6 0.1 collective-permute-start.1
  0.8 0.5 collective-permute-start
  1.2 45.8 %relay_group.1 = (f32[8,7168]{1,0:T(8,128)}, bf16[128,7168]{1,0:T(8,128)(2,1)}) custom-call(bf16[128,7168]{1,0:T(8,128)(2,1)} %bitcast.14, bf16[128,7168]{1,0:T(8,128)(2,1)} %bitcast.19, bf16[8,896,128]{2,1,0:T(8,128)(2,1)} %bitcast.15, bf16[8,896,128]{2,1,0:T(8,128)(2,1)} %bitcast.16, bf16[128,7168]{1,0:T(8,128)(2,1)} %bitcast.17, s32[8,128]{1,0:T(8,128)} %bitcast.22, ...), custom_call_target="tpu_custom_call" | custom-call | flops 880803840 | bytes 12845056 | tf_op jit(solution)/shard_map/relay_group/pallas_call | solution.py:391
  47.0 0.0 collective-permute-done
  47.0 0.0 copy-start.1
  47.0 0.0 collective-permute-done.1.grads_hbm
  47.0 0.0 copy-start
  47.1 0.6 copy-done.1
  47.6 0.7 copy-done
  48.3 56.9 %relay_finish.1 = (bf16[128,7168]{1,0:T(8,128)(2,1)}, bf16[128,7168]{1,0:T(8,128)(2,1)}) custom-call(s32[8,128]{1,0:T(8,128)} %bitcast.23, f32[8,7168]{1,0:T(8,128)} %get-tuple-element.6.rows_hbm, bf16[128,7168]{1,0:T(8,128)(2,1)} %copy-done, bf16[128,7168]{1,0:T(8,128)(2,1)} %get-tuple-element.7.down_hbm), custom_call_target="tpu_custom_call" | custom-call | flops 14680064 | bytes 7340032 | tf_op jit(solution)/shard_map/relay_finish/pallas_call | solution.py:491
Async XLA Ops:
  0.6 46.4 %collective-permute-start.1 = (bf16[128,7168]{1,0:T(8,128)(2,1)}, bf16[128,7168]{1,0:T(8,128)(2,1)S(1)}, u32[]{:S(2)}, u32[]{:S(2)}) collective-permute-start(bf16[128,7168]{1,0:T(8,128)(2,1)} %bitcast.18), channel_id=1, source_target_pairs={{0,16},{16,0},{1,17},{17,1},{2,18},{18,2},{3,19},{19,3},{4,20},{20... | collective-permute-start | bytes 5505032 | tf_op jit(solution)/shard_map/ppermute | solution.py:560
  0.8 46.3 %collective-permute-start = (s32[128,8]{0,1:T(8,128)}, s32[128,8]{0,1:T(8,128)S(1)}, u32[]{:S(2)}, u32[]{:S(2)}) collective-permute-start(s32[128,8]{0,1:T(8,128)} %bitcast.21), channel_id=1, source_target_pairs={{0,16},{16,0},{1,17},{17,1},{2,18},{18,2},{3,19},{19,3},{4,20},{20... | collective-permute-start | bytes 12296 | tf_op jit(solution)/shard_map/ppermute | solution.py:560
  47.0 0.6 copy-start.1
  47.0 1.2 %copy-start = (bf16[128,7168]{1,0:T(8,128)(2,1)}, bf16[128,7168]{1,0:T(8,128)(2,1)S(1)}, u32[]{:S(2)}) copy-start(bf16[128,7168]{1,0:T(8,128)(2,1)S(1)} %collective-permute-done.1.grads_hbm) | copy-start | bytes 5505028

commit v3 on v2

--- a/solution.py
+++ b/solution.py
@@ -47,8 +47,6 @@
     )
     slot = lax.broadcasted_iota(jnp.int32, (8, tok), 0).astype(jnp.float32)
     pick = jnp.where((member8 == 1.0) & (position == slot), 1.0, 0.0)
-    if gate is None:
-        return pick, None
     weight = jnp.sum(jnp.where(hit, gate, 0.0), axis=0, keepdims=True)
     return pick, jnp.sum(pick * weight, axis=1, keepdims=True)
 
@@ -64,10 +62,10 @@
 def group_kernel(
     x_hbm, g_hbm, wg_hbm, wu_hbm, wd_hbm, route_hbm, gate_hbm,
     rows_out, down_out,
-    route_v, gate_v, x_v, g_v, wgu, wd_v, staged, plain, plain_in, gath, xf, gf, pfull, part,
+    route_v, gate_v, pick_v, x_v, g_v, wgu, wd_v, staged, plain, plain_in, gath, xf, gf, pfull, part,
     diag_in, fwd_x, fwd_y, in_x, in_y, zsum, in_z, down_v, rows_v,
     load_sem, out_sem, z_send, z_recv, xy_send, xy_recv, d_send, d_recv, dz_send, dz_recv,
-    p_send, p_recv, s1_send, s1_recv, s2_send, s2_recv, s3_send, s3_recv,
+    p_send, p_recv, t_send, t_recv, s1_send, s1_recv, s2_send, s2_recv, s3_send, s3_recv,
 ):
     slots, piece = staged.shape[0], staged.shape[2]
     block = wd_v.shape[0]
@@ -116,6 +114,7 @@
     for copy in small:
         copy.wait()
     pick, coef = pick_slots(route_v[...], gate_v[...])
+    pick_v[...] = pick
     pick_mat = pick.astype(jnp.bfloat16)
 
     for kind in range(2):
@@ -211,6 +210,10 @@
 
     to_plane(0)
     plain_copy = start(remote(plain_in.at[0], plain_in.at[1], p_send, p_recv, back_dev[0]))
+    width = x_v.shape[1]
+    pick_copy = start(
+        remote(pick_v, rows_v.at[:, pl.ds(width, pick_v.shape[1])], t_send, t_recv, back_dev[0])
+    )
     z_arrived(2)
     to_plane(2)
     to_corner(0)
@@ -350,10 +353,10 @@
             hidden_t, gf[q], preferred_element_type=jnp.float32
         ).astype(jnp.bfloat16)
 
+    send_home(0)
     for q in range(PIECES // 2):
         down_piece(q)
     pass_on(1)
-    send_home(0)
     for q in range(PIECES // 2, PIECES):
         down_piece(q)
     down_copy = pltpu.make_async_copy(down_v, down_out, out_sem.at[0])
@@ -361,7 +364,8 @@
     send_home(1)
 
     plain_copy.wait_recv()
-    rows_v[slots:] = jnp.zeros((rows_v.shape[0] - slots, rows_v.shape[1]), jnp.float32)
+    pick_copy.wait_recv()
+    rows_v[slots:, :width] = jnp.zeros((rows_v.shape[0] - slots, width), jnp.float32)
     for c, (lo, count) in enumerate(chunks):
         for k in range(4):
             homeward(k % 2, c, k).wait_recv()
@@ -391,7 +395,7 @@
     return pl.pallas_call(
         group_kernel,
         out_shape=(
-            jax.ShapeDtypeStruct((8, width), jnp.float32),
+            jax.ShapeDtypeStruct((8, width + tok), jnp.float32),
             jax.ShapeDtypeStruct((block, width), bf16),
         ),
         in_specs=[whole] * 7,
@@ -399,6 +403,7 @@
         scratch_shapes=[
             pltpu.VMEM(route.shape[::-1], jnp.int32),
             pltpu.VMEM(gate.shape[::-1], jnp.float32),
+            pltpu.VMEM((8, tok), jnp.float32),
             pltpu.VMEM((tok, width), bf16),
             pltpu.VMEM((tok, width), bf16),
             pltpu.VMEM((PIECES, piece, 2 * block), bf16),
@@ -419,9 +424,9 @@
             pairs,
             pltpu.VMEM((4, CAP, PIECES, piece), bf16),
             pltpu.VMEM((block, width), bf16),
-            pltpu.VMEM((8, width), jnp.float32),
+            pltpu.VMEM((8, width + tok), jnp.float32),
             dma((5 + 2 * PIECES,)), dma((2,)), dma((4,)), dma((4,)), dma((2, 4, 2)),
-            dma((2, 4, 2)), dma((2, 2)), dma((2, 2)), dma((2,)), dma((2,)), dma, dma,
+            dma((2, 4, 2)), dma((2, 2)), dma((2, 2)), dma((2,)), dma((2,)), dma, dma, dma, dma,
             dma((2, 2, 4)), dma((2, 2, 4)), dma((2, 2, 2)), dma((2, 2, 2)),
             dma((2, 4)), dma((2, 4)),
         ],
@@ -439,36 +444,29 @@
     )
 
 
-def finish_kernel(route_hbm, rows_hbm, grads_hbm, down_hbm, handed_out, down_out,
-                  route_v, rows_v, grads_v, done_v, sem, down_sem):
-    piece = grads_v.shape[1] // PIECES
-
-    def cols(q):
-        return pl.ds(q * piece, piece)
-
-    first = [
-        pltpu.make_async_copy(route_hbm, route_v, sem.at[0]),
-        pltpu.make_async_copy(rows_hbm, rows_v, sem.at[1]),
-    ]
-    loads = [
-        pltpu.make_async_copy(grads_hbm.at[:, cols(q)], grads_v.at[:, cols(q)], sem.at[2 + q])
-        for q in range(PIECES)
-    ]
-    stores = [
-        pltpu.make_async_copy(done_v.at[:, cols(q)], handed_out.at[:, cols(q)],
-                              sem.at[2 + PIECES + q])
-        for q in range(PIECES)
-    ]
-    downs = [
-        pltpu.make_async_copy(down_hbm.at[:, cols(q)], down_out.at[:, cols(q)], down_sem.at[q])
-        for q in range(PIECES)
-    ]
-    for copy in first + loads + downs:
-        copy.start()
-    for copy in first:
-        copy.wait()
-    pick, _ = pick_slots(route_v[...], None)
-    named = jnp.transpose(pick)
+def finish_kernel(rows_hbm, grads_hbm, down_hbm, handed_out, down_out,
+                  rows_v, grads_v, done_v, down_v, rows_sem, sem, down_sem):
+    width = grads_v.shape[1]
+    piece = width // PIECES
+
+    def moves(source, dest, sems, first):
+        return [
+            pltpu.make_async_copy(source.at[:, pl.ds(q * piece, piece)],
+                                  dest.at[:, pl.ds(q * piece, piece)], sems.at[first + q])
+            for q in range(PIECES)
+        ]
+
+    rows_load = pltpu.make_async_copy(rows_hbm, rows_v, rows_sem)
+    loads = moves(grads_hbm, grads_v, sem, 0)
+    stores = moves(done_v, handed_out, sem, PIECES)
+    down_loads = moves(down_hbm, down_v, down_sem, 0)
+    down_stores = moves(down_v, down_out, down_sem, PIECES)
+    rows_load.start()
+    for q in range(PIECES):
+        loads[q].start()
+        down_loads[q].start()
+    rows_load.wait()
+    named = jnp.transpose(rows_v[:, width:])
     changed = jnp.sum(named, axis=1, keepdims=True) > 0.0
     named = named.astype(jnp.bfloat16)
     for q in range(PIECES):
@@ -481,32 +479,36 @@
             jnp.bfloat16
         )
         stores[q].start()
-    for copy in stores + downs:
+        down_loads[q].wait()
+        down_stores[q].start()
+    for copy in stores + down_stores:
         copy.wait()
 
 
-def finish(route, rows, grads, down):
+def finish(rows, grads, down):
     whole = pl.BlockSpec(memory_space=pl.ANY)
     like = jax.ShapeDtypeStruct(grads.shape, grads.dtype)
+    block = pltpu.VMEM(grads.shape, grads.dtype)
     return pl.pallas_call(
         finish_kernel,
         out_shape=(like, jax.ShapeDtypeStruct(down.shape, down.dtype)),
-        in_specs=[whole] * 4,
+        in_specs=[whole] * 3,
         out_specs=(whole, whole),
         scratch_shapes=[
-            pltpu.VMEM(route.shape[::-1], jnp.int32),
             pltpu.VMEM(rows.shape, rows.dtype),
-            pltpu.VMEM(grads.shape, grads.dtype),
-            pltpu.VMEM(grads.shape, grads.dtype),
-            pltpu.SemaphoreType.DMA((2 + 2 * PIECES,)),
-            pltpu.SemaphoreType.DMA((PIECES,)),
+            block,
+            block,
+            pltpu.VMEM(down.shape, down.dtype),
+            pltpu.SemaphoreType.DMA,
+            pltpu.SemaphoreType.DMA((2 * PIECES,)),
+            pltpu.SemaphoreType.DMA((2 * PIECES,)),
         ],
-        compiler_params=pltpu.CompilerParams(vmem_limit_bytes=60 * 2**20),
+        compiler_params=pltpu.CompilerParams(vmem_limit_bytes=121 * 2**19),
         cost_estimate=pl.CostEstimate(
             flops=16 * grads.size, bytes_accessed=8 * grads.size, transcendentals=0
         ),
         name="relay_finish",
-    )(route.T, rows, grads, down)
+    )(rows, grads, down)
 
 
 def plain_work(rows, gate_cols, up_cols, down_rows):
@@ -567,9 +569,8 @@
     live = lax.axis_size("expert") // SHARDS
     if live == 1:
         grads_behind = other_core(grads)
-        route_behind = other_core(route)
         rows, down_part = group_work(inputs, grads, gate_cols, up_cols, down_rows, route, gate)
-        handed, down_part = finish(route_behind, rows, grads_behind, down_part)
+        handed, down_part = finish(rows, grads_behind, down_part)
         return handed[None], down_part[None]
     _, weight, pick = slot_picks(route, gate, live)
     pick_mat = pick.astype(jnp.bfloat16).reshape(tok_rows, live * CAP)

time: 105 us -> 53.3 us (0.51)
  Pallas kernels: 103 us -> 51.1 us
    pallas_call x1, Pallas kernels: 56.9 us -> 5.16 us  [finish(): pl.pallas_call(finish_kernel, out_shape=(like, jax.ShapeDtypeStruct(down....]
  transfers between devices with their start and end apart: 2 -> 1, of which waited for: 0 -> 0; matrix products, arithmetic and copies ran while one was open for 0% -> 0% of each run, Pallas kernels for 44% -> 87%
where the time goes in v3:
time: 53.3 us; the launch traced here: 53.1 us
  Pallas kernels  51.1 us (96%)
  local copies, waits for them, and re-layouts  1.22 us (2%)
  between operations  0.66 us (1%)
    pallas_call x1, Pallas kernels, group_work(): pl.pallas_call(group_kernel, out_shape=(jax.ShapeDtypeStruct((8, width +...  45.9 us
    pallas_call x1, Pallas kernels, finish(): pl.pallas_call(finish_kernel, out_shape=(like, jax.ShapeDtypeStruct(down....  5.16 us
    unnamed x2, local copies, waits for them, and re-layouts  1.22 us
  transfers between devices with their start and end apart: 1, of which 0 were waited for; matrix products, arithmetic and copies ran while one was open for 0% of the time, Pallas kernels for 87%

profile of v3, /device:TPU:1, one launch (start us, length us, event | category | flops | bytes accessed | tf_op | source)
XLA Modules:
  0.0 53.1 jit_solution(9452897405768268396)
XLA Ops:
  0.6 0.1 collective-permute-start
  0.8 45.9 %relay_group.1 = (f32[8,7296]{1,0:T(8,128)}, bf16[128,7168]{1,0:T(8,128)(2,1)}) custom-call(bf16[128,7168]{1,0:T(8,128)(2,1)} %bitcast.13, bf16[128,7168]{1,0:T(8,128)(2,1)} %bitcast.18, bf16[8,896,128]{2,1,0:T(8,128)(2,1)} %bitcast.14, bf16[8,896,128]{2,1,0:T(8,128)(2,1)} %bitcast.15, bf16[128,7168]{1,0:T(8,128)(2,1)} %bitcast.16, s32[8,128]{1,0:T(8,128)} %bitcast.19, ...), custom_call_target="tpu_custom_call" | custom-call | flops 880803840 | bytes 12845056 | tf_op jit(solution)/shard_map/relay_group/pallas_call | solution.py:395
  46.7 0.0 collective-permute-done.grads_hbm
  46.7 0.0 copy-start
  46.7 1.2 %copy-done = bf16[128,7168]{1,0:T(8,128)(2,1)} copy-done((bf16[128,7168]{1,0:T(8,128)(2,1)}, bf16[128,7168]{1,0:T(8,128)(2,1)S(1)}, u32[]{:S(2)}) %copy-start) | copy-done | bytes 1835032
  47.9 5.2 %relay_finish.1 = (bf16[128,7168]{1,0:T(8,128)(2,1)}, bf16[128,7168]{1,0:T(8,128)(2,1)}) custom-call(f32[8,7296]{1,0:T(8,128)} %get-tuple-element.6.rows_hbm, bf16[128,7168]{1,0:T(8,128)(2,1)} %copy-done, bf16[128,7168]{1,0:T(8,128)(2,1)} %get-tuple-element.7.down_hbm), custom_call_target="tpu_custom_call" | custom-call | flops 14680064 | bytes 7340032 | tf_op jit(solution)/shard_map/relay_finish/pallas_call | solution.py:492
Async XLA Ops:
  0.6 46.1 %collective-permute-start = (bf16[128,7168]{1,0:T(8,128)(2,1)}, bf16[128,7168]{1,0:T(8,128)(2,1)S(1)}, u32[]{:S(2)}, u32[]{:S(2)}) collective-permute-start(bf16[128,7168]{1,0:T(8,128)(2,1)} %bitcast.17), channel_id=1, source_target_pairs={{0,16},{16,0},{1,17},{17,1},{2,18},{18,2},{3,19},{19,3},{4,20},{20... | collective-permute-start | bytes 5505032 | tf_op jit(solution)/shard_map/ppermute | solution.py:562
  46.7 1.2 %copy-start = (bf16[128,7168]{1,0:T(8,128)(2,1)}, bf16[128,7168]{1,0:T(8,128)(2,1)S(1)}, u32[]{:S(2)}) copy-start(bf16[128,7168]{1,0:T(8,128)(2,1)S(1)} %collective-permute-done.grads_hbm) | copy-start | bytes 5505028

commit v4 on v3

--- a/solution.py
+++ b/solution.py
@@ -61,11 +61,11 @@
 
 def group_kernel(
     x_hbm, g_hbm, wg_hbm, wu_hbm, wd_hbm, route_hbm, gate_hbm,
-    rows_out, down_out,
+    rows_v, base_v, down_v,
     route_v, gate_v, pick_v, x_v, g_v, wgu, wd_v, staged, plain, plain_in, gath, xf, gf, pfull, part,
-    diag_in, fwd_x, fwd_y, in_x, in_y, zsum, in_z, down_v, rows_v,
-    load_sem, out_sem, z_send, z_recv, xy_send, xy_recv, d_send, d_recv, dz_send, dz_recv,
-    p_send, p_recv, t_send, t_recv, s1_send, s1_recv, s2_send, s2_recv, s3_send, s3_recv,
+    diag_in, fwd_x, fwd_y, in_x, in_y, zsum, in_z,
+    load_sem, z_send, z_recv, xy_send, xy_recv, d_send, d_recv, dz_send, dz_recv,
+    p_send, p_recv, t_send, t_recv, b_send, b_recv, s1_send, s1_recv, s2_send, s2_recv, s3_send, s3_recv,
 ):
     slots, piece = staged.shape[0], staged.shape[2]
     block = wd_v.shape[0]
@@ -214,6 +214,7 @@
     pick_copy = start(
         remote(pick_v, rows_v.at[:, pl.ds(width, pick_v.shape[1])], t_send, t_recv, back_dev[0])
     )
+    base_copy = start(remote(g_v, base_v, b_send, b_recv, back_dev[0]))
     z_arrived(2)
     to_plane(2)
     to_corner(0)
@@ -359,8 +360,6 @@
     pass_on(1)
     for q in range(PIECES // 2, PIECES):
         down_piece(q)
-    down_copy = pltpu.make_async_copy(down_v, down_out, out_sem.at[0])
-    down_copy.start()
     send_home(1)
 
     plain_copy.wait_recv()
@@ -375,12 +374,9 @@
                 total = total + in_z[k, i].astype(jnp.float32)
             for q in range(PIECES):
                 rows_v[i:i + 1, q * piece:(q + 1) * piece] = total[q:q + 1, :]
-    rows_copy = pltpu.make_async_copy(rows_v, rows_out, out_sem.at[1])
-    rows_copy.start()
+    base_copy.wait_recv()
     for copy in sent:
         copy.wait_send()
-    down_copy.wait()
-    rows_copy.wait()
 
 
 def group_work(inputs, grads, gate_cols, up_cols, down_rows, route, gate):
@@ -389,17 +385,19 @@
     piece = width // PIECES
     bf16 = jnp.bfloat16
     whole = pl.BlockSpec(memory_space=pl.ANY)
+    near = pl.BlockSpec(memory_space=pltpu.VMEM)
     dma = pltpu.SemaphoreType.DMA
     pairs = pltpu.VMEM((2, CAP, 2, PIECES, piece), bf16)
     singles = pltpu.VMEM((2, CAP, PIECES, piece), bf16)
     return pl.pallas_call(
         group_kernel,
         out_shape=(
-            jax.ShapeDtypeStruct((8, width + tok), jnp.float32),
-            jax.ShapeDtypeStruct((block, width), bf16),
+            pltpu.VMEM((8, width + tok), jnp.float32),
+            pltpu.VMEM((tok, width), bf16),
+            pltpu.VMEM((block, width), bf16),
         ),
         in_specs=[whole] * 7,
-        out_specs=(whole, whole),
+        out_specs=(near, near, near),
         scratch_shapes=[
             pltpu.VMEM(route.shape[::-1], jnp.int32),
             pltpu.VMEM(gate.shape[::-1], jnp.float32),
@@ -423,49 +421,45 @@
             pairs,
             pairs,
             pltpu.VMEM((4, CAP, PIECES, piece), bf16),
-            pltpu.VMEM((block, width), bf16),
-            pltpu.VMEM((8, width + tok), jnp.float32),
-            dma((5 + 2 * PIECES,)), dma((2,)), dma((4,)), dma((4,)), dma((2, 4, 2)),
+            dma((5 + 2 * PIECES,)), dma((4,)), dma((4,)), dma((2, 4, 2)),
             dma((2, 4, 2)), dma((2, 2)), dma((2, 2)), dma((2,)), dma((2,)), dma, dma, dma, dma,
+            dma, dma,
             dma((2, 2, 4)), dma((2, 2, 4)), dma((2, 2, 2)), dma((2, 2, 2)),
             dma((2, 4)), dma((2, 4)),
         ],
         compiler_params=pltpu.CompilerParams(
-            collective_id=0, has_side_effects=True, vmem_limit_bytes=60 * 2**20
+            collective_id=0, has_side_effects=True, vmem_limit_bytes=40 * 2**20
         ),
         cost_estimate=pl.CostEstimate(
             flops=12 * CAP * SHARDS * width * block, bytes_accessed=14 * tok * width,
             transcendentals=CAP * SHARDS * block,
         ),
         name="relay_group",
-    )(
-        inputs, grads, gate_cols.reshape(PIECES, piece, block),
-        up_cols.reshape(PIECES, piece, block), down_rows, route.T, gate.T,
-    )
-
-
-def finish_kernel(rows_hbm, grads_hbm, down_hbm, handed_out, down_out,
-                  rows_v, grads_v, done_v, down_v, rows_sem, sem, down_sem):
-    width = grads_v.shape[1]
+    )(*(
+        pltpu.with_memory_space_constraint(operand, pltpu.HBM)
+        for operand in (
+            inputs, grads, gate_cols.reshape(PIECES, piece, block),
+            up_cols.reshape(PIECES, piece, block), down_rows, route.T, gate.T,
+        )
+    ))
+
+
+def finish_kernel(rows_v, base_v, down_v, handed_out, down_out, done_v, sem, down_sem):
+    width = base_v.shape[1]
     piece = width // PIECES
-
-    def moves(source, dest, sems, first):
-        return [
-            pltpu.make_async_copy(source.at[:, pl.ds(q * piece, piece)],
-                                  dest.at[:, pl.ds(q * piece, piece)], sems.at[first + q])
-            for q in range(PIECES)
-        ]
-
-    rows_load = pltpu.make_async_copy(rows_hbm, rows_v, rows_sem)
-    loads = moves(grads_hbm, grads_v, sem, 0)
-    stores = moves(done_v, handed_out, sem, PIECES)
-    down_loads = moves(down_hbm, down_v, down_sem, 0)
-    down_stores = moves(down_v, down_out, down_sem, PIECES)
-    rows_load.start()
-    for q in range(PIECES):
-        loads[q].start()
-        down_loads[q].start()
-    rows_load.wait()
+    halves = down_v.shape[0] // 2
+    downs = [
+        pltpu.make_async_copy(down_v.at[pl.ds(h * halves, halves)],
+                              down_out.at[pl.ds(h * halves, halves)], down_sem.at[h])
+        for h in range(2)
+    ]
+    for copy in downs:
+        copy.start()
+    stores = [
+        pltpu.make_async_copy(done_v.at[:, pl.ds(q * piece, piece)],
+                              handed_out.at[:, pl.ds(q * piece, piece)], sem.at[q])
+        for q in range(PIECES)
+    ]
     named = jnp.transpose(rows_v[:, width:])
     changed = jnp.sum(named, axis=1, keepdims=True) > 0.0
     named = named.astype(jnp.bfloat16)
@@ -474,41 +468,36 @@
         placed = jnp.dot(
             named, rows_v[:, at].astype(jnp.bfloat16), preferred_element_type=jnp.float32
         )
-        loads[q].wait()
-        done_v[:, at] = jnp.where(changed, placed, grads_v[:, at].astype(jnp.float32)).astype(
+        done_v[:, at] = jnp.where(changed, placed, base_v[:, at].astype(jnp.float32)).astype(
             jnp.bfloat16
         )
         stores[q].start()
-        down_loads[q].wait()
-        down_stores[q].start()
-    for copy in stores + down_stores:
+    for copy in stores + downs:
         copy.wait()
 
 
-def finish(rows, grads, down):
+def finish(rows, base, down):
     whole = pl.BlockSpec(memory_space=pl.ANY)
-    like = jax.ShapeDtypeStruct(grads.shape, grads.dtype)
-    block = pltpu.VMEM(grads.shape, grads.dtype)
+    near = pl.BlockSpec(memory_space=pltpu.VMEM)
     return pl.pallas_call(
         finish_kernel,
-        out_shape=(like, jax.ShapeDtypeStruct(down.shape, down.dtype)),
-        in_specs=[whole] * 3,
+        out_shape=(
+            jax.ShapeDtypeStruct(base.shape, base.dtype),
+            jax.ShapeDtypeStruct(down.shape, down.dtype),
+        ),
+        in_specs=[near] * 3,
         out_specs=(whole, whole),
         scratch_shapes=[
-            pltpu.VMEM(rows.shape, rows.dtype),
-            block,
-            block,
-            pltpu.VMEM(down.shape, down.dtype),
-            pltpu.SemaphoreType.DMA,
-            pltpu.SemaphoreType.DMA((2 * PIECES,)),
-            pltpu.SemaphoreType.DMA((2 * PIECES,)),
+            pltpu.VMEM(base.shape, base.dtype),
+            pltpu.SemaphoreType.DMA((PIECES,)),
+            pltpu.SemaphoreType.DMA((2,)),
         ],
-        compiler_params=pltpu.CompilerParams(vmem_limit_bytes=121 * 2**19),
+        compiler_params=pltpu.CompilerParams(vmem_limit_bytes=24 * 2**20),
         cost_estimate=pl.CostEstimate(
-            flops=16 * grads.size, bytes_accessed=8 * grads.size, transcendentals=0
+            flops=16 * base.size, bytes_accessed=4 * base.size, transcendentals=0
         ),
         name="relay_finish",
-    )(rows, grads, down)
+    )(rows, base, down)
 
 
 def plain_work(rows, gate_cols, up_cols, down_rows):
@@ -568,9 +557,10 @@
     tok_rows = inputs.shape[0]
     live = lax.axis_size("expert") // SHARDS
     if live == 1:
-        grads_behind = other_core(grads)
-        rows, down_part = group_work(inputs, grads, gate_cols, up_cols, down_rows, route, gate)
-        handed, down_part = finish(rows, grads_behind, down_part)
+        rows, base, down_part = group_work(
+            inputs, grads, gate_cols, up_cols, down_rows, route, gate
+        )
+        handed, down_part = finish(rows, base, down_part)
         return handed[None], down_part[None]
     _, weight, pick = slot_picks(route, gate, live)
     pick_mat = pick.astype(jnp.bfloat16).reshape(tok_rows, live * CAP)

time: 53.3 us -> 47.6 us (0.89)
  Pallas kernels: 51.1 us -> 46.8 us
  local copies, waits for them, and re-layouts: 1.22 us -> 0 us
    pallas_call x2, Pallas kernels: 51.1 us -> 46.8 us  [the longest x1 44.8 us: group_work(): pl.pallas_call(group_kernel, out_shape=(pltpu.VMEM((8, width + tok), jnp....]
    unnamed x2 -> x0, local copies, waits for them, and re-layouts: 1.22 us -> none
  transfers between devices with their start and end apart: 1 -> 0, of which waited for: 0 -> 0; matrix products, arithmetic and copies ran while one was open for 0% -> 0% of each run, Pallas kernels for 87% -> 0%
where the time goes in v4:
time: 47.6 us; the launch traced here: 47.4 us
  Pallas kernels  46.8 us (98%)
  between operations  0.64 us (1%)
    pallas_call x1, Pallas kernels, group_work(): pl.pallas_call(group_kernel, out_shape=(pltpu.VMEM((8, width + tok), jnp....  44.8 us
    pallas_call x1, Pallas kernels, finish(): pl.pallas_call(finish_kernel, out_shape=(jax.ShapeDtypeStruct(base.shape,...  1.92 us

profile of v4, /device:TPU:1, one launch (start us, length us, event | category | flops | bytes accessed | tf_op | source)
XLA Modules:
  0.0 47.4 jit_solution(16759088329155623331)
XLA Ops:
  0.6 44.8 %relay_group.1 = (f32[8,7296]{1,0:T(8,128)S(1)}, bf16[128,7168]{1,0:T(8,128)(2,1)S(1)}, bf16[128,7168]{1,0:T(8,128)(2,1)S(1)}) custom-call(bf16[128,7168]{1,0:T(8,128)(2,1)} %bitcast.13, bf16[128,7168]{1,0:T(8,128)(2,1)} %bitcast.14, bf16[8,896,128]{2,1,0:T(8,128)(2,1)} %bitcast.15, bf16[8,896,128]{2,1,0:T(8,128)(2,1)} %bitcast.16, ...), custom_call_target="tpu_custom_call" | custom-call | flops 880803840 | bytes 12845056 | tf_op jit(solution)/shard_map/relay_group/pallas_call | solution.py:392
  45.5 1.9 %relay_finish.1 = (bf16[128,7168]{1,0:T(8,128)(2,1)}, bf16[128,7168]{1,0:T(8,128)(2,1)}) custom-call(f32[8,7296]{1,0:T(8,128)S(1)} %get-tuple-element.7.rows_v, bf16[128,7168]{1,0:T(8,128)(2,1)S(1)} %get-tuple-element.8.base_v, bf16[128,7168]{1,0:T(8,128)(2,1)S(1)} %get-tuple-element.9.down_v), custom_call_target="tpu_custom_call" | custom-call | flops 14680064 | bytes 3670016 | tf_op jit(solution)/shard_map/relay_finish/pallas_call | solution.py:482

commit v5 on v4

--- a/solution.py
+++ b/solution.py
@@ -105,8 +105,8 @@
         for kind, (src, dst) in enumerate(((x_hbm, x_v), (g_hbm, g_v)))
     ]
     weights = [
-        pltpu.make_async_copy(wg_hbm, wgu.at[:, :, pl.ds(0, block)], load_sem.at[2]),
-        pltpu.make_async_copy(wu_hbm, wgu.at[:, :, pl.ds(block, block)], load_sem.at[3]),
+        pltpu.make_async_copy(wg_hbm, wgu.at[:, pl.ds(0, block)], load_sem.at[2]),
+        pltpu.make_async_copy(wu_hbm, wgu.at[:, pl.ds(block, block)], load_sem.at[3]),
         pltpu.make_async_copy(wd_hbm, wd_v, load_sem.at[4]),
     ]
     for copy in small + row_loads[0] + row_loads[1]:
@@ -117,6 +117,63 @@
     pick_v[...] = pick
     pick_mat = pick.astype(jnp.bfloat16)
 
+    def index(spot, k):
+        return (k % 2) * 8 + spot * 2 + lax.rem(z // 2 + k // 2, 2)
+
+    own = index(xy, 0)
+
+    def remote(src, dst, send, recv, to):
+        return pltpu.make_async_remote_copy(
+            src_ref=src, dst_ref=dst, send_sem=send, recv_sem=recv, device_id=to,
+            device_id_type=MESH,
+        )
+
+    sent = []
+
+    def start(copy):
+        copy.start()
+        sent.append(copy)
+        return copy
+
+    def slab(spot, k, kind):
+        return gath.at[kind, index(spot, k)]
+
+    def over_z(kind):
+        for k in (2, 1, 3):
+            start(remote(slab(xy, 0, kind), gath.at[kind, (k % 2) * 8 + xy * 2 + z // 2],
+                         z_send.at[k, kind], z_recv.at[k, kind], z_dev[k]))
+
+    def to_plane(k, kind):
+        ref = slab(xy, k, kind)
+        for axis, to in ((kind, (x_dev, y_dev)[kind]), (1 - kind, (y_dev, x_dev)[kind])):
+            start(remote(ref, ref, xy_send.at[axis, k, kind], xy_recv.at[axis, k, kind], to))
+
+    def arrived(axis, k, kind):
+        ref = slab(at_x if axis == 0 else at_y, k, kind)
+        remote(ref, ref, xy_send.at[axis, k, kind], xy_recv.at[axis, k, kind], x_dev).wait_recv()
+
+    def to_corner(k):
+        for kind, (spot, to) in enumerate(((at_x, y_dev), (at_y, x_dev))):
+            arrived(kind, k, kind)
+            ref = slab(spot, k, kind)
+            start(remote(ref, ref, d_send.at[k // 2, kind], d_recv.at[k // 2, kind], to))
+
+    def z_arrived(k, kind):
+        ref = slab(xy, k, kind)
+        remote(ref, ref, z_send.at[k, kind], z_recv.at[k, kind], z_dev[k]).wait_recv()
+
+    def corner_over_z(k, kind):
+        source = index(at_d, k)
+        return remote(gath.at[kind, source], gath.at[kind, 8 + source], dz_send.at[k // 2, kind],
+                      dz_recv.at[k // 2, kind], z_dev[1])
+
+    def corner_passed(k):
+        for kind in range(2):
+            ref = slab(at_d, k, kind)
+            remote(ref, ref, d_send.at[k // 2, kind], d_recv.at[k // 2, kind], y_dev).wait_recv()
+            start(corner_over_z(k, kind))
+
+    tiles = piece // 128
     for kind in range(2):
         source = x_v if kind == 0 else g_v
         for q in range(PIECES):
@@ -126,128 +183,65 @@
             )
             scaled = rows if kind == 0 else rows * coef
             for i in range(slots):
-                staged[i, kind * PIECES + q:kind * PIECES + q + 1, :] = scaled[i:i + 1, :]
+                staged[i, q:q + 1, :] = scaled[i:i + 1, :]
                 if kind == 1:
-                    plain[i, q:q + 1, :] = rows[i:i + 1, :]
-
-    def index(spot, k):
-        return (k % 2) * 8 + spot * 2 + lax.rem(z // 2 + k // 2, 2)
-
-    own = index(xy, 0)
-    for i in range(slots):
-        gath[own, i] = staged[i].astype(jnp.bfloat16)
+                    for m in range(tiles):
+                        j, sub = divmod(q * tiles + m, PIECES)
+                        plain[i, sub:sub + 1, j * 128:(j + 1) * 128] = rows[
+                            i:i + 1, m * 128:(m + 1) * 128
+                        ]
+        for i in range(slots):
+            gath[kind, own, i] = staged[i].astype(jnp.bfloat16)
+        if kind == 0:
+            pl.semaphore_wait(barrier, 9)
+        over_z(kind)
+        to_plane(0, kind)
     plain_in[0] = plain[...].astype(jnp.bfloat16)
     for copy in weights:
         copy.start()
-    pl.semaphore_wait(barrier, 9)
-
-    def remote(src, dst, send, recv, to):
-        return pltpu.make_async_remote_copy(
-            src_ref=src, dst_ref=dst, send_sem=send, recv_sem=recv, device_id=to,
-            device_id_type=MESH,
-        )
-
-    sent = []
-
-    def start(copy):
-        copy.start()
-        sent.append(copy)
-        return copy
-
-    for k in (2, 1, 3):
-        start(remote(gath.at[own], gath.at[(k % 2) * 8 + xy * 2 + z // 2],
-                     z_send.at[k], z_recv.at[k], z_dev[k]))
-
-    def halves(k):
-        if k % 2 == 1:
-            return (pl.ds(0, slots),)
-        cut = 3 if k == 0 else 2
-        return (pl.ds(0, cut), pl.ds(cut, slots - cut))
-
-    def slab(spot, k, half):
-        return gath.at[index(spot, k), halves(k)[half]]
-
-    def over(axis, k, half):
-        ref = slab(xy, k, half)
-        return remote(ref, ref, xy_send.at[axis, k, half], xy_recv.at[axis, k, half],
-                      x_dev if axis == 0 else y_dev)
-
-    def to_plane(k):
-        if k % 2 == 1:
-            start(over(0, k, 0))
-            start(over(1, k, 0))
-        else:
-            start(over(0, k, 0))
-            start(over(1, k, 1))
-            start(over(0, k, 1))
-            start(over(1, k, 0))
-
-    def arrived(axis, k, half):
-        ref = slab(at_x if axis == 0 else at_y, k, half)
-        remote(ref, ref, xy_send.at[axis, k, half], xy_recv.at[axis, k, half], x_dev).wait_recv()
-
-    def to_corner(k):
-        arrived(0, k, 0)
-        ref = slab(at_x, k, 0)
-        start(remote(ref, ref, d_send.at[k // 2, 0], d_recv.at[k // 2, 0], y_dev))
-        arrived(1, k, 1)
-        ref = slab(at_y, k, 1)
-        start(remote(ref, ref, d_send.at[k // 2, 1], d_recv.at[k // 2, 1], x_dev))
-
-    def corner_arrived(k):
-        for half in range(2):
-            ref = slab(at_d, k, half)
-            remote(ref, ref, d_send.at[k // 2, half], d_recv.at[k // 2, half], y_dev).wait_recv()
-
-    def z_arrived(k):
-        ref = gath.at[index(xy, k)]
-        remote(ref, ref, z_send.at[k], z_recv.at[k], z_dev[k]).wait_recv()
-
-    def corner_over_z(k):
-        source = index(at_d, k)
-        return remote(gath.at[source], gath.at[8 + source], dz_send.at[k // 2],
-                      dz_recv.at[k // 2], z_dev[1])
-
-    to_plane(0)
     plain_copy = start(remote(plain_in.at[0], plain_in.at[1], p_send, p_recv, back_dev[0]))
     width = x_v.shape[1]
     pick_copy = start(
         remote(pick_v, rows_v.at[:, pl.ds(width, pick_v.shape[1])], t_send, t_recv, back_dev[0])
     )
     base_copy = start(remote(g_v, base_v, b_send, b_recv, back_dev[0]))
-    z_arrived(2)
-    to_plane(2)
+    for kind in range(2):
+        z_arrived(2, kind)
+        to_plane(2, kind)
     to_corner(0)
     to_corner(2)
-    z_arrived(1)
-    to_plane(1)
-    corner_arrived(0)
-    start(corner_over_z(0))
-    z_arrived(3)
-    to_plane(3)
-    corner_arrived(2)
-    start(corner_over_z(2))
+    for kind in range(2):
+        z_arrived(1, kind)
+        to_plane(1, kind)
+    corner_passed(0)
+    for kind in range(2):
+        z_arrived(3, kind)
+        to_plane(3, kind)
+    corner_passed(2)
 
     group_rows = slots * 8
-    to_rows = swap_order(8, 2 * PIECES)
+    to_rows = swap_order(8, PIECES)
     to_units = swap_order(PIECES, 8)
-    chunks = ((0, 3), (3, slots - 3))
+    chunks = ((0, (tiles + 1) // 2), ((tiles + 1) // 2, tiles // 2))
 
     def compute(r):
         for i in range(slots):
-            packed = gath[r * 8:(r + 1) * 8, i].reshape(8 * 2 * PIECES, piece)
-            ordered = jnp.dot(to_rows, packed, preferred_element_type=jnp.float32)
             at = r * group_rows + i * 8
-            for q in range(PIECES):
-                xf[q, at:at + 8, :] = ordered[q * 8:(q + 1) * 8].astype(jnp.bfloat16)
-                gf[q, at:at + 8, :] = ordered[
-                    (PIECES + q) * 8:(PIECES + q + 1) * 8
-                ].astype(jnp.bfloat16)
+            for kind, out in enumerate((xf, gf)):
+                packed = gath[kind, r * 8:(r + 1) * 8, i].astype(jnp.float32)
+                ordered = jnp.dot(
+                    to_rows, packed.reshape(8 * PIECES, piece).astype(jnp.bfloat16),
+                    preferred_element_type=jnp.float32,
+                )
+                for q in range(PIECES):
+                    out[q, at:at + 8, :] = ordered[q * 8:(q + 1) * 8].astype(jnp.bfloat16)
         mine = slice(r * group_rows, (r + 1) * group_rows)
         pre = jnp.zeros((group_rows, 2 * block), jnp.float32)
         back = jnp.zeros((group_rows, block), jnp.float32)
         for q in range(PIECES):
-            pre = pre + jnp.dot(xf[q, mine, :], wgu[q], preferred_element_type=jnp.float32)
+            pre = pre + jnp.dot(
+                xf[q, mine, :], wgu[q * piece:(q + 1) * piece, :], preferred_element_type=jnp.float32
+            )
             back = back + lax.dot_general(
                 gf[q, mine, :], wd_v[:, q * piece:(q + 1) * piece], CONTRACT_LAST,
                 preferred_element_type=jnp.float32,
@@ -260,73 +254,85 @@
 
     def diagonal(r, c, half):
         lo, count = chunks[c]
-        at = pl.ds(lo, count)
-        return remote(part.at[r, at, at_d, half], diag_in.at[r, at, half],
+        at = pl.ds(lo * 128, count * 128)
+        return remote(part.at[r, :, at_d, half, :, at], diag_in.at[r, :, half, :, at],
                       s1_send.at[r, c, half], s1_recv.at[r, c, half],
                       y_dev if half == 0 else x_dev)
 
     def direct(r, c, half):
         lo, count = chunks[c]
-        at = pl.ds(lo, count)
+        at = pl.ds(lo * 128, count * 128)
         if half == 1:
-            return remote(part.at[r, at, at_x, 1], in_x.at[r, at, 1], s1_send.at[r, c, 2],
+            return remote(part.at[r, :, at_x, 1, :, at], in_x.at[r, :, 1, :, at], s1_send.at[r, c, 2],
                           s1_recv.at[r, c, 2], x_dev)
-        return remote(part.at[r, at, at_y, 0], in_y.at[r, at, 0], s1_send.at[r, c, 3],
+        return remote(part.at[r, :, at_y, 0, :, at], in_y.at[r, :, 0, :, at], s1_send.at[r, c, 3],
                       s1_recv.at[r, c, 3], y_dev)
 
     def passed(r, c, half):
         lo, count = chunks[c]
-        at = pl.ds(lo, count)
+        at = pl.ds(lo * 128, count * 128)
         if half == 0:
-            return remote(fwd_x.at[r, at], in_x.at[r, at, 0], s2_send.at[r, c, 0],
+            return remote(fwd_x.at[r, :, :, at], in_x.at[r, :, 0, :, at], s2_send.at[r, c, 0],
                           s2_recv.at[r, c, 0], x_dev)
-        return remote(fwd_y.at[r, at], in_y.at[r, at, 1], s2_send.at[r, c, 1],
+        return remote(fwd_y.at[r, :, :, at], in_y.at[r, :, 1, :, at], s2_send.at[r, c, 1],
                       s2_recv.at[r, c, 1], y_dev)
 
     def homeward(r, c, k):
         lo, count = chunks[c]
-        at = pl.ds(lo, count)
-        return remote(zsum.at[r, at, lax.rem(z // 2 + k // 2, 2)], in_z.at[k, at],
+        at = pl.ds(lo * 128, count * 128)
+        return remote(zsum.at[r, :, lax.rem(z // 2 + k // 2, 2), :, at], in_z.at[k, :, :, at],
                       s3_send.at[c, k], s3_recv.at[c, k], back_dev[k])
 
     def send_shares(r, grad_both):
-        for q in range(PIECES):
-            share = lax.dot_general(
-                grad_both, wgu[q], CONTRACT_LAST, preferred_element_type=jnp.float32
-            ).astype(jnp.bfloat16)
+        for c, (lo, count) in enumerate(chunks):
+            lanes = slice(lo * 128, (lo + count) * 128)
+            for j in range(lo, lo + count):
+                wide = PIECES * 128
+                share = lax.dot_general(
+                    grad_both, wgu[j * wide:(j + 1) * wide, :], CONTRACT_LAST,
+                    preferred_element_type=jnp.float32,
+                ).astype(jnp.bfloat16)
+                for i in range(slots):
+                    for q in range(PIECES):
+                        pfull[r, i, q * 8:(q + 1) * 8, j * 128:(j + 1) * 128] = share[
+                            i * 8:(i + 1) * 8, q * 128:(q + 1) * 128
+                        ]
             for i in range(slots):
-                pfull[r, i, q * 8:(q + 1) * 8, :] = share[i * 8:(i + 1) * 8]
-        for c, (lo, count) in enumerate(chunks):
-            for i in range(lo, lo + count):
-                units = jnp.dot(to_units, pfull[r, i], preferred_element_type=jnp.float32)
-                part[r, i] = units.reshape(4, 2, PIECES, piece).astype(jnp.bfloat16)
+                units = jnp.dot(
+                    to_units, pfull[r, i, :, lanes], preferred_element_type=jnp.float32
+                )
+                part[r, i, :, :, :, lanes] = units.reshape(
+                    4, 2, PIECES, count * 128
+                ).astype(jnp.bfloat16)
             for half in range(2):
                 start(diagonal(r, c, half))
-        for c in range(2):
             for half in range(2):
                 start(direct(r, c, half))
 
     def pass_on(r):
         for c, (lo, count) in enumerate(chunks):
+            lanes = slice(lo * 128, (lo + count) * 128)
             for half in range(2):
                 diagonal(r, c, half).wait_recv()
                 spot, out = (at_x, fwd_x) if half == 0 else (at_y, fwd_y)
-                for i in range(lo, lo + count):
-                    out[r, i] = (
-                        part[r, i, spot, half].astype(jnp.float32)
-                        + diag_in[r, i, half].astype(jnp.float32)
+                for i in range(slots):
+                    out[r, i, :, lanes] = (
+                        part[r, i, spot, half, :, lanes].astype(jnp.float32)
+                        + diag_in[r, i, half, :, lanes].astype(jnp.float32)
                     ).astype(jnp.bfloat16)
                 start(passed(r, c, half))
 
     def send_home(r):
         for c, (lo, count) in enumerate(chunks):
+            lanes = slice(lo * 128, (lo + count) * 128)
             for half in range(2):
                 direct(r, c, half).wait_recv()
                 passed(r, c, half).wait_recv()
-            for i in range(lo, lo + count):
-                zsum[r, i] = (
-                    part[r, i, xy].astype(jnp.float32) + in_x[r, i].astype(jnp.float32)
-                    + in_y[r, i].astype(jnp.float32)
+            for i in range(slots):
+                zsum[r, i, :, :, lanes] = (
+                    part[r, i, xy, :, :, lanes].astype(jnp.float32)
+                    + in_x[r, i, :, :, lanes].astype(jnp.float32)
+                    + in_y[r, i, :, :, lanes].astype(jnp.float32)
                 ).astype(jnp.bfloat16)
             for k in (r + 2, r):
                 start(homeward(r, c, k))
@@ -340,10 +346,12 @@
     hidden_a, grad_both = compute(0)
     send_shares(0, grad_both)
     for k in (1, 3):
-        arrived(0, k, 0)
-        arrived(1, k, 0)
+        for kind in range(2):
+            arrived(0, k, kind)
+            arrived(1, k, kind)
     for k in (0, 2):
-        corner_over_z(k).wait_recv()
+        for kind in range(2):
+            corner_over_z(k, kind).wait_recv()
     hidden_b, grad_both = compute(1)
     pass_on(0)
     send_shares(1, grad_both)
@@ -368,12 +376,15 @@
     for c, (lo, count) in enumerate(chunks):
         for k in range(4):
             homeward(k % 2, c, k).wait_recv()
-        for i in range(lo, lo + count):
-            total = plain_in[1, i].astype(jnp.float32)
+        lanes = slice(lo * 128, (lo + count) * 128)
+        for i in range(slots):
+            total = plain_in[1, i, :, lanes].astype(jnp.float32)
             for k in range(4):
-                total = total + in_z[k, i].astype(jnp.float32)
-            for q in range(PIECES):
-                rows_v[i:i + 1, q * piece:(q + 1) * piece] = total[q:q + 1, :]
+                total = total + in_z[k, i, :, lanes].astype(jnp.float32)
+            for j in range(count):
+                for q in range(PIECES):
+                    at = ((lo + j) * PIECES + q) * 128
+                    rows_v[i:i + 1, at:at + 128] = total[q:q + 1, j * 128:(j + 1) * 128]
     base_copy.wait_recv()
     for copy in sent:
         copy.wait_send()
@@ -404,12 +415,12 @@
             pltpu.VMEM((8, tok), jnp.float32),
             pltpu.VMEM((tok, width), bf16),
             pltpu.VMEM((tok, width), bf16),
-            pltpu.VMEM((PIECES, piece, 2 * block), bf16),
+            pltpu.VMEM((width, 2 * block), bf16),
             pltpu.VMEM((block, width), bf16),
-            pltpu.VMEM((CAP, 2 * PIECES, piece), jnp.float32),
+            pltpu.VMEM((CAP, PIECES, piece), jnp.float32),
             pltpu.VMEM((CAP, PIECES, piece), jnp.float32),
             singles,
-            pltpu.VMEM((SHARDS, CAP, 2 * PIECES, piece), bf16),
+            pltpu.VMEM((2, SHARDS, CAP, PIECES, piece), bf16),
             pltpu.VMEM((PIECES, CAP * SHARDS, piece), bf16),
             pltpu.VMEM((PIECES, CAP * SHARDS, piece), bf16),
             pltpu.VMEM((2, CAP, 8 * PIECES, piece), bf16),
@@ -421,8 +432,8 @@
             pairs,
             pairs,
             pltpu.VMEM((4, CAP, PIECES, piece), bf16),
-            dma((5 + 2 * PIECES,)), dma((4,)), dma((4,)), dma((2, 4, 2)),
-            dma((2, 4, 2)), dma((2, 2)), dma((2, 2)), dma((2,)), dma((2,)), dma, dma, dma, dma,
+            dma((5 + 2 * PIECES,)), dma((4, 2)), dma((4, 2)), dma((2, 4, 2)),
+            dma((2, 4, 2)), dma((2, 2)), dma((2, 2)), dma((2, 2)), dma((2, 2)), dma, dma, dma, dma,
             dma, dma,
             dma((2, 2, 4)), dma((2, 2, 4)), dma((2, 2, 2)), dma((2, 2, 2)),
             dma((2, 4)), dma((2, 4)),
@@ -438,8 +449,7 @@
     )(*(
         pltpu.with_memory_space_constraint(operand, pltpu.HBM)
         for operand in (
-            inputs, grads, gate_cols.reshape(PIECES, piece, block),
-            up_cols.reshape(PIECES, piece, block), down_rows, route.T, gate.T,
+            inputs, grads, gate_cols, up_cols, down_rows, route.T, gate.T,
         )
     ))
 

time: 47.6 us -> 50.3 us (1.057)
  Pallas kernels: 46.8 us -> 49.4 us
    pallas_call x1, Pallas kernels: 44.8 us -> 47.5 us  [group_work(): pl.pallas_call(group_kernel, out_shape=(pltpu.VMEM((8, width + tok), jnp....]
where the time goes in v5:
time: 50.3 us; the launch traced here: 50.1 us
  Pallas kernels  49.4 us (98%)
  between operations  0.64 us (1%)
    pallas_call x1, Pallas kernels, group_work(): pl.pallas_call(group_kernel, out_shape=(pltpu.VMEM((8, width + tok), jnp....  47.5 us
    pallas_call x1, Pallas kernels, finish(): pl.pallas_call(finish_kernel, out_shape=(jax.ShapeDtypeStruct(base.shape,...  1.92 us

profile of v5, /device:TPU:1, one launch (start us, length us, event | category | flops | bytes accessed | tf_op | source)
XLA Modules:
  0.0 50.1 jit_solution(9853522591693392017)
XLA Ops:
  0.6 47.5 %relay_group.1 = (f32[8,7296]{1,0:T(8,128)S(1)}, bf16[128,7168]{1,0:T(8,128)(2,1)S(1)}, bf16[128,7168]{1,0:T(8,128)(2,1)S(1)}) custom-call(bf16[128,7168]{1,0:T(8,128)(2,1)} %bitcast.13, bf16[128,7168]{1,0:T(8,128)(2,1)} %bitcast.14, bf16[7168,128]{1,0:T(8,128)(2,1)} %bitcast.15, bf16[7168,128]{1,0:T(8,128)(2,1)} %bitcast.16, bf16[128,7168]{1,0:T(8,128)(2,1)} %bitcast.17, ...), custom_call_target="tpu_custom_call" | custom-call | flops 880803840 | bytes 12845056 | tf_op jit(solution)/shard_map/relay_group/pallas_call | solution.py:403
  48.1 1.9 %relay_finish.1 = (bf16[128,7168]{1,0:T(8,128)(2,1)}, bf16[128,7168]{1,0:T(8,128)(2,1)}) custom-call(f32[8,7296]{1,0:T(8,128)S(1)} %get-tuple-element.7.rows_v, bf16[128,7168]{1,0:T(8,128)(2,1)S(1)} %get-tuple-element.8.base_v, bf16[128,7168]{1,0:T(8,128)(2,1)S(1)} %get-tuple-element.9.down_v), custom_call_target="tpu_custom_call" | custom-call | flops 14680064 | bytes 3670016 | tf_op jit(solution)/shard_map/relay_finish/pallas_call | solution.py:492

commit v6 on v5

--- a/solution.py
+++ b/solution.py
@@ -173,7 +173,6 @@
             remote(ref, ref, d_send.at[k // 2, kind], d_recv.at[k // 2, kind], y_dev).wait_recv()
             start(corner_over_z(k, kind))
 
-    tiles = piece // 128
     for kind in range(2):
         source = x_v if kind == 0 else g_v
         for q in range(PIECES):
@@ -185,11 +184,7 @@
             for i in range(slots):
                 staged[i, q:q + 1, :] = scaled[i:i + 1, :]
                 if kind == 1:
-                    for m in range(tiles):
-                        j, sub = divmod(q * tiles + m, PIECES)
-                        plain[i, sub:sub + 1, j * 128:(j + 1) * 128] = rows[
-                            i:i + 1, m * 128:(m + 1) * 128
-                        ]
+                    plain[i, q:q + 1, :] = rows[i:i + 1, :]
         for i in range(slots):
             gath[kind, own, i] = staged[i].astype(jnp.bfloat16)
         if kind == 0:
@@ -222,7 +217,7 @@
     group_rows = slots * 8
     to_rows = swap_order(8, PIECES)
     to_units = swap_order(PIECES, 8)
-    chunks = ((0, (tiles + 1) // 2), ((tiles + 1) // 2, tiles // 2))
+    chunks = ((0, 3), (3, slots - 3))
 
     def compute(r):
         for i in range(slots):
@@ -254,85 +249,73 @@
 
     def diagonal(r, c, half):
         lo, count = chunks[c]
-        at = pl.ds(lo * 128, count * 128)
-        return remote(part.at[r, :, at_d, half, :, at], diag_in.at[r, :, half, :, at],
+        at = pl.ds(lo, count)
+        return remote(part.at[r, at, at_d, half], diag_in.at[r, at, half],
                       s1_send.at[r, c, half], s1_recv.at[r, c, half],
                       y_dev if half == 0 else x_dev)
 
     def direct(r, c, half):
         lo, count = chunks[c]
-        at = pl.ds(lo * 128, count * 128)
+        at = pl.ds(lo, count)
         if half == 1:
-            return remote(part.at[r, :, at_x, 1, :, at], in_x.at[r, :, 1, :, at], s1_send.at[r, c, 2],
+            return remote(part.at[r, at, at_x, 1], in_x.at[r, at, 1], s1_send.at[r, c, 2],
                           s1_recv.at[r, c, 2], x_dev)
-        return remote(part.at[r, :, at_y, 0, :, at], in_y.at[r, :, 0, :, at], s1_send.at[r, c, 3],
+        return remote(part.at[r, at, at_y, 0], in_y.at[r, at, 0], s1_send.at[r, c, 3],
                       s1_recv.at[r, c, 3], y_dev)
 
     def passed(r, c, half):
         lo, count = chunks[c]
-        at = pl.ds(lo * 128, count * 128)
+        at = pl.ds(lo, count)
         if half == 0:
-            return remote(fwd_x.at[r, :, :, at], in_x.at[r, :, 0, :, at], s2_send.at[r, c, 0],
+            return remote(fwd_x.at[r, at], in_x.at[r, at, 0], s2_send.at[r, c, 0],
                           s2_recv.at[r, c, 0], x_dev)
-        return remote(fwd_y.at[r, :, :, at], in_y.at[r, :, 1, :, at], s2_send.at[r, c, 1],
+        return remote(fwd_y.at[r, at], in_y.at[r, at, 1], s2_send.at[r, c, 1],
                       s2_recv.at[r, c, 1], y_dev)
 
     def homeward(r, c, k):
         lo, count = chunks[c]
-        at = pl.ds(lo * 128, count * 128)
-        return remote(zsum.at[r, :, lax.rem(z // 2 + k // 2, 2), :, at], in_z.at[k, :, :, at],
+        at = pl.ds(lo, count)
+        return remote(zsum.at[r, at, lax.rem(z // 2 + k // 2, 2)], in_z.at[k, at],
                       s3_send.at[c, k], s3_recv.at[c, k], back_dev[k])
 
     def send_shares(r, grad_both):
+        for q in range(PIECES):
+            share = lax.dot_general(
+                grad_both, wgu[q * piece:(q + 1) * piece, :], CONTRACT_LAST, preferred_element_type=jnp.float32
+            ).astype(jnp.bfloat16)
+            for i in range(slots):
+                pfull[r, i, q * 8:(q + 1) * 8, :] = share[i * 8:(i + 1) * 8]
         for c, (lo, count) in enumerate(chunks):
-            lanes = slice(lo * 128, (lo + count) * 128)
-            for j in range(lo, lo + count):
-                wide = PIECES * 128
-                share = lax.dot_general(
-                    grad_both, wgu[j * wide:(j + 1) * wide, :], CONTRACT_LAST,
-                    preferred_element_type=jnp.float32,
-                ).astype(jnp.bfloat16)
-                for i in range(slots):
-                    for q in range(PIECES):
-                        pfull[r, i, q * 8:(q + 1) * 8, j * 128:(j + 1) * 128] = share[
-                            i * 8:(i + 1) * 8, q * 128:(q + 1) * 128
-                        ]
-            for i in range(slots):
-                units = jnp.dot(
-                    to_units, pfull[r, i, :, lanes], preferred_element_type=jnp.float32
-                )
-                part[r, i, :, :, :, lanes] = units.reshape(
-                    4, 2, PIECES, count * 128
-                ).astype(jnp.bfloat16)
+            for i in range(lo, lo + count):
+                units = jnp.dot(to_units, pfull[r, i], preferred_element_type=jnp.float32)
+                part[r, i] = units.reshape(4, 2, PIECES, piece).astype(jnp.bfloat16)
             for half in range(2):
                 start(diagonal(r, c, half))
+        for c in range(2):
             for half in range(2):
                 start(direct(r, c, half))
 
     def pass_on(r):
         for c, (lo, count) in enumerate(chunks):
-            lanes = slice(lo * 128, (lo + count) * 128)
             for half in range(2):
                 diagonal(r, c, half).wait_recv()
                 spot, out = (at_x, fwd_x) if half == 0 else (at_y, fwd_y)
-                for i in range(slots):
-                    out[r, i, :, lanes] = (
-                        part[r, i, spot, half, :, lanes].astype(jnp.float32)
-                        + diag_in[r, i, half, :, lanes].astype(jnp.float32)
+                for i in range(lo, lo + count):
+                    out[r, i] = (
+                        part[r, i, spot, half].astype(jnp.float32)
+                        + diag_in[r, i, half].astype(jnp.float32)
                     ).astype(jnp.bfloat16)
                 start(passed(r, c, half))
 
     def send_home(r):
         for c, (lo, count) in enumerate(chunks):
-            lanes = slice(lo * 128, (lo + count) * 128)
             for half in range(2):
                 direct(r, c, half).wait_recv()
                 passed(r, c, half).wait_recv()
-            for i in range(slots):
-                zsum[r, i, :, :, lanes] = (
-                    part[r, i, xy, :, :, lanes].astype(jnp.float32)
-                    + in_x[r, i, :, :, lanes].astype(jnp.float32)
-                    + in_y[r, i, :, :, lanes].astype(jnp.float32)
+            for i in range(lo, lo + count):
+                zsum[r, i] = (
+                    part[r, i, xy].astype(jnp.float32) + in_x[r, i].astype(jnp.float32)
+                    + in_y[r, i].astype(jnp.float32)
                 ).astype(jnp.bfloat16)
             for k in (r + 2, r):
                 start(homeward(r, c, k))
@@ -376,15 +359,12 @@
     for c, (lo, count) in enumerate(chunks):
         for k in range(4):
             homeward(k % 2, c, k).wait_recv()
-        lanes = slice(lo * 128, (lo + count) * 128)
-        for i in range(slots):
-            total = plain_in[1, i, :, lanes].astype(jnp.float32)
+        for i in range(lo, lo + count):
+            total = plain_in[1, i].astype(jnp.float32)
             for k in range(4):
-                total = total + in_z[k, i, :, lanes].astype(jnp.float32)
-            for j in range(count):
-                for q in range(PIECES):
-                    at = ((lo + j) * PIECES + q) * 128
-                    rows_v[i:i + 1, at:at + 128] = total[q:q + 1, j * 128:(j + 1) * 128]
+                total = total + in_z[k, i].astype(jnp.float32)
+            for q in range(PIECES):
+                rows_v[i:i + 1, q * piece:(q + 1) * piece] = total[q:q + 1, :]
     base_copy.wait_recv()
     for copy in sent:
         copy.wait_send()

time: 50.3 us -> 50.5 us (level)
  no operation moved by 1% of the time
where the time goes in v6:
time: 50.5 us; the launch traced here: 50.3 us
  Pallas kernels  49.7 us (98%)
  between operations  0.64 us (1%)
    pallas_call x1, Pallas kernels, group_work(): pl.pallas_call(group_kernel, out_shape=(pltpu.VMEM((8, width + tok), jnp....  47.7 us
    pallas_call x1, Pallas kernels, finish(): pl.pallas_call(finish_kernel, out_shape=(jax.ShapeDtypeStruct(base.shape,...  1.92 us

profile of v6, /device:TPU:1, one launch (start us, length us, event | category | flops | bytes accessed | tf_op | source)
XLA Modules:
  0.0 50.3 jit_solution(7227764462904198884)
XLA Ops:
  0.6 47.7 %relay_group.1 = (f32[8,7296]{1,0:T(8,128)S(1)}, bf16[128,7168]{1,0:T(8,128)(2,1)S(1)}, bf16[128,7168]{1,0:T(8,128)(2,1)S(1)}) custom-call(bf16[128,7168]{1,0:T(8,128)(2,1)} %bitcast.13, bf16[128,7168]{1,0:T(8,128)(2,1)} %bitcast.14, bf16[7168,128]{1,0:T(8,128)(2,1)} %bitcast.15, bf16[7168,128]{1,0:T(8,128)(2,1)} %bitcast.16, bf16[128,7168]{1,0:T(8,128)(2,1)} %bitcast.17, ...), custom_call_target="tpu_custom_call" | custom-call | flops 880803840 | bytes 12845056 | tf_op jit(solution)/shard_map/relay_group/pallas_call | solution.py:383
  48.4 1.9 %relay_finish.1 = (bf16[128,7168]{1,0:T(8,128)(2,1)}, bf16[128,7168]{1,0:T(8,128)(2,1)}) custom-call(f32[8,7296]{1,0:T(8,128)S(1)} %get-tuple-element.7.rows_v, bf16[128,7168]{1,0:T(8,128)(2,1)S(1)} %get-tuple-element.8.base_v, bf16[128,7168]{1,0:T(8,128)(2,1)S(1)} %get-tuple-element.9.down_v), custom_call_target="tpu_custom_call" | custom-call | flops 14680064 | bytes 3670016 | tf_op jit(solution)/shard_map/relay_finish/pallas_call | solution.py:472

commit v7 on v4

--- a/solution.py
+++ b/solution.py
@@ -214,7 +214,6 @@
     pick_copy = start(
         remote(pick_v, rows_v.at[:, pl.ds(width, pick_v.shape[1])], t_send, t_recv, back_dev[0])
     )
-    base_copy = start(remote(g_v, base_v, b_send, b_recv, back_dev[0]))
     z_arrived(2)
     to_plane(2)
     to_corner(0)
@@ -344,6 +343,7 @@
         arrived(1, k, 0)
     for k in (0, 2):
         corner_over_z(k).wait_recv()
+    base_copy = start(remote(g_v, base_v, b_send, b_recv, back_dev[0]))
     hidden_b, grad_both = compute(1)
     pass_on(0)
     send_shares(1, grad_both)
@@ -355,12 +355,14 @@
         ).astype(jnp.bfloat16)
 
     send_home(0)
-    for q in range(PIECES // 2):
+    for q in range(2):
         down_piece(q)
     pass_on(1)
-    for q in range(PIECES // 2, PIECES):
+    for q in range(2, 5):
         down_piece(q)
     send_home(1)
+    for q in range(5, PIECES):
+        down_piece(q)
 
     plain_copy.wait_recv()
     pick_copy.wait_recv()

time: 47.6 us -> 47.6 us (level)
  no operation moved by 1% of the time
where the time goes in v7:
time: 47.6 us; the launch traced here: 47.4 us
  Pallas kernels  46.8 us (98%)
  between operations  0.64 us (1%)
    pallas_call x1, Pallas kernels, group_work(): pl.pallas_call(group_kernel, out_shape=(pltpu.VMEM((8, width + tok), jnp....  44.8 us
    pallas_call x1, Pallas kernels, finish(): pl.pallas_call(finish_kernel, out_shape=(jax.ShapeDtypeStruct(base.shape,...  1.92 us

profile of v7, /device:TPU:1, one launch (start us, length us, event | category | flops | bytes accessed | tf_op | source)
XLA Modules:
  0.0 47.4 jit_solution(8556981659683858368)
XLA Ops:
  0.6 44.8 %relay_group.1 = (f32[8,7296]{1,0:T(8,128)S(1)}, bf16[128,7168]{1,0:T(8,128)(2,1)S(1)}, bf16[128,7168]{1,0:T(8,128)(2,1)S(1)}) custom-call(bf16[128,7168]{1,0:T(8,128)(2,1)} %bitcast.13, bf16[128,7168]{1,0:T(8,128)(2,1)} %bitcast.14, bf16[8,896,128]{2,1,0:T(8,128)(2,1)} %bitcast.15, bf16[8,896,128]{2,1,0:T(8,128)(2,1)} %bitcast.16, ...), custom_call_target="tpu_custom_call" | custom-call | flops 880803840 | bytes 12845056 | tf_op jit(solution)/shard_map/relay_group/pallas_call | solution.py:394
  45.5 1.9 %relay_finish.1 = (bf16[128,7168]{1,0:T(8,128)(2,1)}, bf16[128,7168]{1,0:T(8,128)(2,1)}) custom-call(f32[8,7296]{1,0:T(8,128)S(1)} %get-tuple-element.7.rows_v, bf16[128,7168]{1,0:T(8,128)(2,1)S(1)} %get-tuple-element.8.base_v, bf16[128,7168]{1,0:T(8,128)(2,1)S(1)} %get-tuple-element.9.down_v), custom_call_target="tpu_custom_call" | custom-call | flops 14680064 | bytes 3670016 | tf_op jit(solution)/shard_map/relay_finish/pallas_call | solution.py:484
